TPU v7x, 32 devices: a whole 2x2x4 slice. The times are simulated.
32 devices in a mesh: ctx: 16 (over z, y, core), wsh: 2 (over x).
Axes of the slice: x: 2, y: 2, z: 4, core: 2. Of those that a mesh axis runs over, the one named last changes fastest.
Arguments:
- tokens: bfloat16 [2, 2048, 768], P('wsh', 'ctx'), may hold values from -6 to 6
- doc_ids: int32 [2, 2048], P('wsh', 'ctx'), may hold values from 0 to 7, never falling along the last dimension, each value on 1 to 512 neighbouring positions
- w_qkv: bfloat16 [768, 2304], P('wsh'), may hold values from -0.21875 to 0.21875
- b_query: bfloat16 [768], P('wsh'), may hold values from -3 to 3
- b_value: bfloat16 [768], P('wsh'), may hold values from -3 to 3
- w_out: bfloat16 [768, 768], P('wsh'), may hold values from -0.875 to 0.875
- b_out: bfloat16 [768], P('wsh'), may hold values from -2 to 2
- ln1_gain: bfloat16 [768], P('wsh'), may hold values from 0.5 to 1.5
- ln1_bias: bfloat16 [768], P('wsh'), may hold values from -2 to 2
- w_in: bfloat16 [768, 3072], P('wsh'), may hold values from -0.21875 to 0.21875
- b_in: bfloat16 [3072], P('wsh'), may hold values from -3 to 3
- w_back: bfloat16 [3072, 768], P('wsh'), may hold values from -0.109375 to 0.109375
- b_back: bfloat16 [768], P('wsh'), may hold values from -2 to 2
- ln2_gain: bfloat16 [768], P('wsh'), may hold values from 0.5 to 1.5
- ln2_bias: bfloat16 [768], P('wsh'), may hold values from -2 to 2
- d_out: bfloat16 [2, 2048, 768], P('wsh', 'ctx'), may hold values from -6 to 6
Outputs:
- output: bfloat16 [2, 2048, 768], P('wsh', 'ctx')
- d_tokens: float32 [2, 2048, 768], P('wsh', 'ctx')
- d_w_qkv: float32 [768, 2304], P('wsh')
- d_b_query: float32 [768], P('wsh')
- d_b_value: float32 [768], P('wsh')
- d_w_out: float32 [768, 768], P('wsh')
- d_b_out: float32 [768], P('wsh')
- d_ln1_gain: float32 [768], P('wsh')
- d_ln1_bias: float32 [768], P('wsh')
- d_w_in: float32 [768, 3072], P('wsh')
- d_b_in: float32 [3072], P('wsh')
- d_w_back: float32 [3072, 768], P('wsh')
- d_b_back: float32 [768], P('wsh')
- d_ln2_gain: float32 [768], P('wsh')
- d_ln2_bias: float32 [768], P('wsh')
Inputs may be any that keep to these rules, and one draw needn't show every extreme that they name: `doc_ids`: along each sequence the ids never fall; each document has 1 to 512 tokens and one has exactly 512.
All inputs are finite; a program needn't handle non-finite values.
Results may differ from a plain program's by a relative error of at most 0.019.
Values may be sent and summed in bfloat16 or wider, within the bound.
A program may use at most 192 MiB of HBM per device.

v0:
```python
import jax
import jax.numpy as jnp
from jax import lax
from jax.sharding import PartitionSpec as P

HEADS = 12
HEAD_DIM = 64
SPAN = 4


EPSILON = 1e-05
NEGATIVE = -1e30
ROOT_HALF = 0.7071067811865476
INV_ROOT_TAU = 0.3989422804014327


def passed_along(value, axis, by):
    length = lax.axis_size(axis)
    return lax.ppermute(value, axis, [(i, (i + by) % length) for i in range(length)])


def layer_norm(hidden, gain, offset):
    center = hidden - jnp.mean(hidden, -1, keepdims=True)
    inverse = lax.rsqrt(jnp.mean(center * center, -1, keepdims=True) + EPSILON)
    normed = center * inverse
    return (normed * gain + offset, normed, inverse)


def norm_back(upstream, normed, inverse, gain):
    scaled = upstream * gain
    return inverse * (
        scaled
        - jnp.mean(scaled, -1, keepdims=True)
        - normed * jnp.mean(scaled * normed, -1, keepdims=True)
    )


def score_block(queries, far_keys, q_docs, far_docs):
    raw_dots = jnp.einsum("qhd,khd->hqk", queries, far_keys, preferred_element_type=jnp.float32)
    same_doc = (q_docs[:, None] == far_docs[None, :])[None]
    return (jnp.where(same_doc, raw_dots * HEAD_DIM ** (-0.5), NEGATIVE), same_doc)


def guarded_call(visitor):

    def guarded_visit(carry_in, travel):
        return visitor(carry_in, travel)

    return guarded_visit


def start_blocks(blocks):
    return passed_along((blocks[0], blocks[1], blocks[2]), "ctx", -SPAN)


def fold_blocks(blocks, visitor, carry_in):
    travel = start_blocks(blocks)

    def one_turn(turn_index, state):
        carry_now, travel_now = state
        carry_now = visitor(carry_now, travel_now)
        travel_now = passed_along((travel_now[0], travel_now[1], travel_now[2]), "ctx", 1)
        return (carry_now, travel_now)

    carry_in, travel = lax.fori_loop(0, 2 * SPAN, one_turn, (carry_in, travel))
    return visitor(carry_in, travel)


def body(
    tokens,
    doc_ids,
    w_qkv,
    b_query,
    b_value,
    w_out,
    b_out,
    ln1_gain,
    ln1_bias,
    w_in,
    b_in,
    w_back,
    b_back,
    ln2_gain,
    ln2_bias,
    d_out,
):
    gathered = (
        lax.all_gather(w_qkv, "wsh", axis=0, tiled=True),
        lax.all_gather(b_query, "wsh", axis=0, tiled=True),
        lax.all_gather(b_value, "wsh", axis=0, tiled=True),
        lax.all_gather(w_out, "wsh", axis=0, tiled=True),
        lax.all_gather(b_out, "wsh", axis=0, tiled=True),
        lax.all_gather(ln1_gain, "wsh", axis=0, tiled=True),
        lax.all_gather(ln1_bias, "wsh", axis=0, tiled=True),
        lax.all_gather(w_in, "wsh", axis=0, tiled=True),
        lax.all_gather(b_in, "wsh", axis=0, tiled=True),
        lax.all_gather(w_back, "wsh", axis=0, tiled=True),
        lax.all_gather(b_back, "wsh", axis=0, tiled=True),
        lax.all_gather(ln2_gain, "wsh", axis=0, tiled=True),
        lax.all_gather(ln2_bias, "wsh", axis=0, tiled=True),
    )
    (
        full_qkv,
        full_bq,
        full_bv,
        full_out,
        full_bo,
        gain_one,
        offset_one,
        full_in,
        full_bi,
        full_back,
        full_bb,
        gain_two,
        offset_two,
    ) = gathered
    full_bq = full_bq.astype(jnp.float32)
    full_bv = full_bv.astype(jnp.float32)
    full_bo = full_bo.astype(jnp.float32)
    gain_one = gain_one.astype(jnp.float32)
    offset_one = offset_one.astype(jnp.float32)
    full_bi = full_bi.astype(jnp.float32)
    full_bb = full_bb.astype(jnp.float32)
    gain_two = gain_two.astype(jnp.float32)
    offset_two = offset_two.astype(jnp.float32)
    hidden = tokens[0]
    hidden_f = hidden.astype(jnp.float32)
    tok_count = hidden.shape[0]
    model_width = hidden.shape[1]
    att_scale = HEAD_DIM ** (-0.5)
    head_shape = (tok_count, HEADS, HEAD_DIM)
    q_docs = doc_ids[0].astype(jnp.bfloat16)
    bias_qkv = jnp.concatenate([full_bq, jnp.zeros((model_width,), jnp.float32), full_bv])
    packed = (jnp.dot(hidden, full_qkv, preferred_element_type=jnp.float32) + bias_qkv).astype(
        jnp.bfloat16
    )
    queries = packed[:, :model_width].reshape(head_shape)
    keys = packed[:, model_width : 2 * model_width].reshape(head_shape)
    values = packed[:, 2 * model_width :].reshape(head_shape)
    blocks = (keys, values, q_docs)

    def online_visit(carry_now, travel):
        peak, summed, acc_now = carry_now
        masked, same_doc = score_block(queries, travel[0], q_docs, travel[2])
        new_peak = jnp.maximum(peak, jnp.max(masked, -1))
        weights = jnp.where(same_doc, jnp.exp(masked - new_peak[..., None]), 0.0)
        factor = jnp.exp(peak - new_peak)
        acc_now = acc_now * factor.T[:, :, None] + jnp.einsum(
            "hqk,khd->qhd",
            weights.astype(jnp.bfloat16),
            travel[1],
            preferred_element_type=jnp.float32,
        )
        return (new_peak, summed * factor + jnp.sum(weights, -1), acc_now)

    start_peak = jnp.full((HEADS, tok_count), NEGATIVE, jnp.float32)
    start_sum = jnp.zeros((HEADS, tok_count), jnp.float32)
    start_acc = jnp.zeros(head_shape, jnp.float32)
    peak, summed, acc_end = fold_blocks(
        blocks, guarded_call(online_visit), (start_peak, start_sum, start_acc)
    )
    log_total = peak + jnp.log(summed)
    attn_full = acc_end / summed.T[:, :, None]
    attended = attn_full.reshape(tok_count, model_width).astype(jnp.bfloat16)
    first = hidden_f + jnp.dot(attended, full_out, preferred_element_type=jnp.float32) + full_bo
    normed_one, unit_one, inverse_one = layer_norm(first, gain_one, offset_one)
    normed_low = normed_one.astype(jnp.bfloat16)
    inner = jnp.dot(normed_low, full_in, preferred_element_type=jnp.float32) + full_bi
    erf_part = lax.erf(inner * ROOT_HALF)
    activation = (0.5 * inner * (1.0 + erf_part)).astype(jnp.bfloat16)
    second = (
        normed_one + jnp.dot(activation, full_back, preferred_element_type=jnp.float32) + full_bb
    )
    result, unit_two, inverse_two = layer_norm(second, gain_two, offset_two)
    upstream = d_out[0].astype(jnp.float32)
    d_gain_two = jnp.sum(upstream * unit_two, 0)
    d_offset_two = jnp.sum(upstream, 0)
    d_second = norm_back(upstream, unit_two, inverse_two, gain_two)
    d_second_low = d_second.astype(jnp.bfloat16)
    d_bias_back = jnp.sum(d_second, 0)
    d_weight_back = jnp.einsum(
        "tf,td->fd", activation, d_second_low, preferred_element_type=jnp.float32
    )
    slope = 0.5 * (1.0 + erf_part) + inner * jnp.exp(-0.5 * inner * inner) * INV_ROOT_TAU
    d_inner = jnp.dot(d_second_low, full_back.T, preferred_element_type=jnp.float32) * slope
    d_inner_low = d_inner.astype(jnp.bfloat16)
    d_bias_in = jnp.sum(d_inner, 0)
    d_weight_in = jnp.einsum(
        "td,tf->df", normed_low, d_inner_low, preferred_element_type=jnp.float32
    )
    d_normed = d_second + jnp.dot(d_inner_low, full_in.T, preferred_element_type=jnp.float32)
    d_gain_one = jnp.sum(d_normed * unit_one, 0)
    d_offset_one = jnp.sum(d_normed, 0)
    d_first = norm_back(d_normed, unit_one, inverse_one, gain_one)
    d_first_low = d_first.astype(jnp.bfloat16)
    d_bias_out = jnp.sum(d_first, 0)
    d_weight_out = jnp.einsum(
        "td,te->de", attended, d_first_low, preferred_element_type=jnp.float32
    )
    d_attn = jnp.dot(d_first_low, full_out.T, preferred_element_type=jnp.float32).astype(
        jnp.bfloat16
    )
    d_attn = d_attn.reshape(head_shape)
    delta = jnp.einsum("qhd,qhd->hq", d_attn.astype(jnp.float32), attn_full)
    zeros_head = jnp.zeros(head_shape, jnp.float32)

    def back_visit(carry_now, travel):
        grad_query, grad_key, grad_value = carry_now
        far_keys, far_values, far_docs = travel
        masked, same_doc = score_block(queries, far_keys, q_docs, far_docs)
        probs = jnp.where(same_doc, jnp.exp(masked - log_total[..., None]), 0.0)
        d_probs = jnp.einsum("qhd,khd->hqk", d_attn, far_values, preferred_element_type=jnp.float32)
        d_score = (probs * (d_probs - delta[..., None]) * att_scale).astype(jnp.bfloat16)
        grad_query = grad_query + jnp.einsum(
            "hqk,khd->qhd", d_score, far_keys, preferred_element_type=jnp.float32
        )
        grad_key = grad_key + jnp.einsum(
            "hqk,qhd->khd", d_score, queries, preferred_element_type=jnp.float32
        )
        grad_value = grad_value + jnp.einsum(
            "hqk,qhd->khd", probs.astype(jnp.bfloat16), d_attn, preferred_element_type=jnp.float32
        )
        return (grad_query, grad_key, grad_value)

    back_guarded = guarded_call(back_visit)
    travel = start_blocks(blocks)

    def back_turn(turn_index, state):
        carry_now, travel_now = state
        carry_now = back_guarded(carry_now, travel_now)
        travel_now = passed_along((travel_now[0], travel_now[1], travel_now[2]), "ctx", 1)
        moved = (
            passed_along(carry_now[1].astype(jnp.bfloat16), "ctx", 1).astype(jnp.float32),
            passed_along(carry_now[2].astype(jnp.bfloat16), "ctx", 1).astype(jnp.float32),
        )
        return ((carry_now[0], moved[0], moved[1]), travel_now)

    carry_end, travel = lax.fori_loop(
        0, 2 * SPAN, back_turn, ((zeros_head, zeros_head, zeros_head), travel)
    )
    grad_query, grad_key, grad_value = back_guarded(carry_end, travel)
    grad_key, grad_value = (
        passed_along(grad_key.astype(jnp.bfloat16), "ctx", -SPAN).astype(grad_key.dtype),
        passed_along(grad_value.astype(jnp.bfloat16), "ctx", -SPAN).astype(grad_value.dtype),
    )
    d_packed = jnp.concatenate(
        [
            grad_query.reshape(tok_count, model_width),
            grad_key.reshape(tok_count, model_width),
            grad_value.reshape(tok_count, model_width),
        ],
        1,
    ).astype(jnp.bfloat16)
    d_packed_f = d_packed.astype(jnp.float32)
    d_bias_query = jnp.sum(d_packed_f[:, :model_width], 0)
    d_bias_value = jnp.sum(d_packed_f[:, 2 * model_width :], 0)
    d_weight_qkv = jnp.einsum("td,te->de", hidden, d_packed, preferred_element_type=jnp.float32)
    d_hidden = d_first + jnp.dot(d_packed, full_qkv.T, preferred_element_type=jnp.float32)
    grad_list = [
        d_weight_qkv,
        d_bias_query,
        d_bias_value,
        d_weight_out,
        d_bias_out,
        d_gain_one,
        d_offset_one,
        d_weight_in,
        d_bias_in,
        d_weight_back,
        d_bias_back,
        d_gain_two,
        d_offset_two,
    ]
    group_size = lax.axis_size("wsh")
    ctx_count = lax.axis_size("ctx")
    flat_grads = jnp.concatenate([grad_full.reshape(group_size, -1) for grad_full in grad_list], 1)
    flat_width = flat_grads.shape[1]
    piece_len = -(-flat_width // ctx_count)
    own_shard = (
        lax.psum_scatter(flat_grads.astype(jnp.bfloat16), "wsh", scatter_dimension=0, tiled=True)
        .astype(jnp.float32)
        .reshape(-1)
    )
    spread_shard = own_shard
    spread_shard = spread_shard.reshape(ctx_count, piece_len)
    own_part = lax.psum_scatter(spread_shard, "ctx", scatter_dimension=0, tiled=True)
    summed_flat = (
        lax.all_gather(own_part.astype(jnp.bfloat16), "ctx", axis=0, tiled=True)
        .astype(own_part.dtype)
        .reshape(-1)
    )
    offset = 0
    shards = []
    for grad_full in grad_list:
        length = grad_full.size // group_size
        shard_shape = (grad_full.shape[0] // group_size,) + grad_full.shape[1:]
        shards.append(summed_flat[offset : offset + length].reshape(shard_shape))
        offset = offset + length
    return (result.astype(jnp.bfloat16)[None], d_hidden[None]) + tuple(shards)


def solution(mesh):
    in_specs = (
        P("wsh", "ctx", None),
        P("wsh", "ctx"),
        P("wsh", None),
        P("wsh"),
        P("wsh"),
        P("wsh", None),
        P("wsh"),
        P("wsh"),
        P("wsh"),
        P("wsh", None),
        P("wsh"),
        P("wsh", None),
        P("wsh"),
        P("wsh"),
        P("wsh"),
        P("wsh", "ctx", None),
    )
    out_specs = (
        P("wsh", "ctx", None),
        P("wsh", "ctx", None),
        P("wsh", None),
        P("wsh"),
        P("wsh"),
        P("wsh", None),
        P("wsh"),
        P("wsh"),
        P("wsh"),
        P("wsh", None),
        P("wsh"),
        P("wsh", None),
        P("wsh"),
        P("wsh"),
        P("wsh"),
    )
    return jax.shard_map(body, mesh=mesh, in_specs=in_specs, out_specs=out_specs, check_vma=False)
```

profile of v0, /device:TPU:0, one launch (start us, length us, event | category | flops | bytes accessed | tf_op | source)
XLA Modules:
  0.0 1579.5 jit_solution(13324289869575702522)
XLA Ops:
  51.7 10.3 all-gather.16.cloned.1.call-done
  78.1 80.3 %while.42 = (s32[]{:T(128)}, f32[12,128]{1,0:T(8,128)S(1)}, f32[12,128]{1,0:T(8,128)S(1)}, f32[128,12,64]{0,2,1:T(8,128)S(1)}, bf16[128,12,64]{0,2,1:T(8,128)(2,...) while((s32[]{:T(128)}, f32[12,128]{1,0:T(8,128)S(1)}, ...), condition=%wide.region_3.4_spmd.clone, body=%wide.region_0.3_spmd.clone.sunk | while | flops 52421632 | bytes 6260977 | solution.py:65
  80.8 7.3 collective-permute-done.2
  89.2 8.9 collective-permute-done.2
  99.3 8.9 collective-permute-done.2
  109.3 8.9 collective-permute-done.2
  119.4 8.9 collective-permute-done.2
  129.4 8.9 collective-permute-done.2
  139.4 8.9 collective-permute-done.2
  149.5 8.9 collective-permute-done.2
  166.9 47.7 %all-gather.22.cloned.1.call-done = bf16[3072,768]{1,0:T(8,128)(2,1)} async-done(((bf16[1536,768]{1,0:T(8,128)(2,1)}), bf16[3072,768]{1,0:T(8,128)(2,1)}) %all-gather.22.cloned.1.call-update) | async-done | bytes 4718608 | tf_op jit(solution)/shard_map/all_gather | solution.py:97
  227.6 158.4 %while.43 = (s32[]{:T(128)}, f32[128,12,64]{0,2,1:T(8,128)S(1)}, f32[128,12,64]{0,2,1:T(8,128)}, f32[128,12,64]{0,2,1:T(8,128)}, bf16[128,12,64]{0,2,1:T(8,128)(...) while((s32[]{:T(128)}, f32[128,12,64]{0,2,1:T(8,128)S(1)}, ...), condition=%wide.region_15.16_spmd.clone, body=%wide.region_14.15_spmd.clone.sunk | while | flops 128598016 | bytes 13613429 | solution.py:238
  407.3 7.9 reshape.311
  432.5 7.4 constant_dynamic-update-slice_fusion.12
  459.0 317.9 %all-reduce.5.cloned.1.call-done = bf16[2,3543552]{1,0:T(2,128)(2,1)} async-done(((bf16[2,3543552]{1,0:T(2,128)(2,1)}), bf16[2,3543552]{1,0:T(2,128)(2,1)}) %all-reduce.5.cloned.1.call-update) | async-done | bytes 14174224
  776.9 129.9 %fusion.24 = f32[3543552]{0:T(1024)} fusion(bf16[2,3543552]{1,0:T(2,128)(2,1)} %all-reduce.5.cloned.1.call-done, u32[]{:T(128)} %bitcast.33), kind=kLoop, calls=%fused_computation.39 | loop fusion | flops 3543552 | bytes 21261316 | tf_op jit(solution)/shard_map/reshape;reshape | solution.py:285
  906.8 18.8 %reshape.320 = f32[16,221472]{1,0:T(8,128)} reshape(f32[3543552]{0:T(1024)} %fusion.24) | data formatting | bytes 28348416 | tf_op jit(solution)/shard_map/reshape;reshape | solution.py:285
  925.6 297.7 %all-reduce.6 = bf16[16,221472]{1,0:T(8,128)(2,1)} all-reduce(f32[16,221472]{1,0:T(8,128)} %reshape.320), channel_id=3, replica_groups=mesh['ctx'=16,'wsh'=2] {'ctx'}, use_global_device_ids=true, to_apply=%region_26.27.clone | all-reduce | flops 3543552 | bytes 21261312
  1230.6 112.0 %all-gather.24.cloned.1.call-done = bf16[16,1,221472]{2,1,0:T(2,128)(2,1)} async-done(((bf16[1,1,221472]{2,1,0:T(2,128)(2,1)}), bf16[16,1,221472]{2,1,0:T(2,128)(2,1)}) %all-gather.24.cloned.1.call-update) | async-done | bytes 7087120 | tf_op jit(solution)/shard_map/all_gather | solution.py:288
  1342.6 152.8 %convert_reduce_fusion = f32[16,221472]{1,0:T(8,128)} fusion(bf16[16,1,221472]{2,1,0:T(2,128)(2,1)} %all-gather.24.cloned.1.call-done), kind=kLoop, calls=%fused_computation.37 | loop fusion | flops 3543552 | bytes 21261312 | tf_op jit(solution)/shard_map/convert_element_type | solution.py:289
  1495.3 18.0 %reshape.371 = f32[3543552]{0:T(1024)} reshape(f32[16,221472]{1,0:T(8,128)} %convert_reduce_fusion) | data formatting | bytes 28348416
  1513.3 15.8 %slice.65 = f32[1538,2304]{1,0:T(8,128)} reshape(f32[3543552]{0:T(1024)} %reshape.371) | data formatting | bytes 28348416 | tf_op jit(solution)/shard_map/slice | solution.py:297
  1530.6 16.0 %slice.69 = f32[4614,768]{1,0:T(8,128)} reshape(f32[3543552]{0:T(1024)} %reshape.371) | data formatting | bytes 28348416 | tf_op jit(solution)/shard_map/slice | solution.py:297
  1546.6 6.4 fusion.81
  (581 shorter events, 334.7 us)
Async XLA Ops:
  7.3 54.7 %all-gather.16.cloned.1.call-start = ((), (), s32[]{:S(2)}) async-start(), calls=%async_computation | async-start | bytes 5308416 | tf_op jit(solution)/shard_map/all_gather | solution.py:88
  8.0 153.1 %all-gather.18.cloned.1.call-start = ((), (), s32[]{:S(2)}) async-start(), calls=%async_computation.1 | async-start | bytes 1769472 | tf_op jit(solution)/shard_map/all_gather | solution.py:91
  8.8 154.5 %all-gather.20.cloned.1.call-start = ((), (), s32[]{:S(2)}) async-start(), calls=%async_computation.2 | async-start | bytes 7077888 | tf_op jit(solution)/shard_map/all_gather | solution.py:95
  9.5 205.1 %all-gather.22.cloned.1.call-start = ((), (), s32[]{:S(2)}) async-start(), calls=%async_computation.3 | async-start | bytes 7077888 | tf_op jit(solution)/shard_map/all_gather | solution.py:97
  9.6 65.8 %collective-permute-start.10 = (bf16[128]{0:T(256)(128)(2,1)S(1)}, bf16[128]{0:T(256)(128)(2,1)}, u32[]{:S(2)}, u32[]{:S(2)}) collective-permute-start(bf16[128]{0:T(256)(128)(2,1)S(1)} %convert_bitcast_fusion), channel_id=1, source_target_pairs={{0,24},{2,26},{4,28},{6,30},{8,0},{10,2},{12,4},{14,6},{16,8},{18,... | collective-permute-start | bytes 776 | tf_op jit(solution)/shard_map/ppermute | solution.py:19
  14.7 762.1 %all-reduce.5.cloned.1.call-start = ((), (), s32[]{:S(2)}) async-start(), calls=%async_computation.5 | async-start | bytes 28348416
  228.5 19.5 %collective-permute-start.5 = (bf16[128,12,64]{0,2,1:T(8,128)(2,1)S(1)}, bf16[128,12,64]{0,2,1:T(8,128)(2,1)}, u32[]{:S(2)}, u32[]{:S(2)}) collective-permute-start(bf16[128,12,64]{0,2,1:T(8,128)(2,1)S(1)} %copy.120), channel_id=1, source_target_pairs={{0,2},{2,4},{4,6},{6,8},{8,10},{10,12},{12,14},{14,16},{16,18},{18... | collective-permute-start | bytes 589832 | tf_op jit(solution)/shard_map/while/body/eval_jaxpr/ppermute | solution.py:19
  229.4 18.5 %collective-permute-start.6 = (bf16[128,12,64]{0,2,1:T(8,128)(2,1)S(1)}, bf16[128,12,64]{0,2,1:T(8,128)(2,1)}, u32[]{:S(2)}, u32[]{:S(2)}) collective-permute-start(bf16[128,12,64]{0,2,1:T(8,128)(2,1)S(1)} %copy.121), channel_id=1, source_target_pairs={{0,2},{2,4},{4,6},{6,8},{8,10},{10,12},{12,14},{14,16},{16,18},{18... | collective-permute-start | bytes 589832 | tf_op jit(solution)/shard_map/while/body/eval_jaxpr/ppermute | solution.py:19
  248.9 18.6 %collective-permute-start.5 = (bf16[128,12,64]{0,2,1:T(8,128)(2,1)S(1)}, bf16[128,12,64]{0,2,1:T(8,128)(2,1)}, u32[]{:S(2)}, u32[]{:S(2)}) collective-permute-start(bf16[128,12,64]{0,2,1:T(8,128)(2,1)S(1)} %copy.120), channel_id=1, source_target_pairs={{0,2},{2,4},{4,6},{6,8},{8,10},{10,12},{12,14},{14,16},{16,18},{18... | collective-permute-start | bytes 589832 | tf_op jit(solution)/shard_map/while/body/eval_jaxpr/ppermute | solution.py:19
  249.9 17.7 %collective-permute-start.6 = (bf16[128,12,64]{0,2,1:T(8,128)(2,1)S(1)}, bf16[128,12,64]{0,2,1:T(8,128)(2,1)}, u32[]{:S(2)}, u32[]{:S(2)}) collective-permute-start(bf16[128,12,64]{0,2,1:T(8,128)(2,1)S(1)} %copy.121), channel_id=1, source_target_pairs={{0,2},{2,4},{4,6},{6,8},{8,10},{10,12},{12,14},{14,16},{16,18},{18... | collective-permute-start | bytes 589832 | tf_op jit(solution)/shard_map/while/body/eval_jaxpr/ppermute | solution.py:19
  268.5 18.6 %collective-permute-start.5 = (bf16[128,12,64]{0,2,1:T(8,128)(2,1)S(1)}, bf16[128,12,64]{0,2,1:T(8,128)(2,1)}, u32[]{:S(2)}, u32[]{:S(2)}) collective-permute-start(bf16[128,12,64]{0,2,1:T(8,128)(2,1)S(1)} %copy.120), channel_id=1, source_target_pairs={{0,2},{2,4},{4,6},{6,8},{8,10},{10,12},{12,14},{14,16},{16,18},{18... | collective-permute-start | bytes 589832 | tf_op jit(solution)/shard_map/while/body/eval_jaxpr/ppermute | solution.py:19
  269.5 17.7 %collective-permute-start.6 = (bf16[128,12,64]{0,2,1:T(8,128)(2,1)S(1)}, bf16[128,12,64]{0,2,1:T(8,128)(2,1)}, u32[]{:S(2)}, u32[]{:S(2)}) collective-permute-start(bf16[128,12,64]{0,2,1:T(8,128)(2,1)S(1)} %copy.121), channel_id=1, source_target_pairs={{0,2},{2,4},{4,6},{6,8},{8,10},{10,12},{12,14},{14,16},{16,18},{18... | collective-permute-start | bytes 589832 | tf_op jit(solution)/shard_map/while/body/eval_jaxpr/ppermute | solution.py:19
  288.1 18.5 %collective-permute-start.5 = (bf16[128,12,64]{0,2,1:T(8,128)(2,1)S(1)}, bf16[128,12,64]{0,2,1:T(8,128)(2,1)}, u32[]{:S(2)}, u32[]{:S(2)}) collective-permute-start(bf16[128,12,64]{0,2,1:T(8,128)(2,1)S(1)} %copy.120), channel_id=1, source_target_pairs={{0,2},{2,4},{4,6},{6,8},{8,10},{10,12},{12,14},{14,16},{16,18},{18... | collective-permute-start | bytes 589832 | tf_op jit(solution)/shard_map/while/body/eval_jaxpr/ppermute | solution.py:19
  289.1 17.5 %collective-permute-start.6 = (bf16[128,12,64]{0,2,1:T(8,128)(2,1)S(1)}, bf16[128,12,64]{0,2,1:T(8,128)(2,1)}, u32[]{:S(2)}, u32[]{:S(2)}) collective-permute-start(bf16[128,12,64]{0,2,1:T(8,128)(2,1)S(1)} %copy.121), channel_id=1, source_target_pairs={{0,2},{2,4},{4,6},{6,8},{8,10},{10,12},{12,14},{14,16},{16,18},{18... | collective-permute-start | bytes 589832 | tf_op jit(solution)/shard_map/while/body/eval_jaxpr/ppermute | solution.py:19
  307.5 19.6 %collective-permute-start.5 = (bf16[128,12,64]{0,2,1:T(8,128)(2,1)S(1)}, bf16[128,12,64]{0,2,1:T(8,128)(2,1)}, u32[]{:S(2)}, u32[]{:S(2)}) collective-permute-start(bf16[128,12,64]{0,2,1:T(8,128)(2,1)S(1)} %copy.120), channel_id=1, source_target_pairs={{0,2},{2,4},{4,6},{6,8},{8,10},{10,12},{12,14},{14,16},{16,18},{18... | collective-permute-start | bytes 589832 | tf_op jit(solution)/shard_map/while/body/eval_jaxpr/ppermute | solution.py:19
  308.5 18.7 %collective-permute-start.6 = (bf16[128,12,64]{0,2,1:T(8,128)(2,1)S(1)}, bf16[128,12,64]{0,2,1:T(8,128)(2,1)}, u32[]{:S(2)}, u32[]{:S(2)}) collective-permute-start(bf16[128,12,64]{0,2,1:T(8,128)(2,1)S(1)} %copy.121), channel_id=1, source_target_pairs={{0,2},{2,4},{4,6},{6,8},{8,10},{10,12},{12,14},{14,16},{16,18},{18... | collective-permute-start | bytes 589832 | tf_op jit(solution)/shard_map/while/body/eval_jaxpr/ppermute | solution.py:19
  328.1 18.6 %collective-permute-start.5 = (bf16[128,12,64]{0,2,1:T(8,128)(2,1)S(1)}, bf16[128,12,64]{0,2,1:T(8,128)(2,1)}, u32[]{:S(2)}, u32[]{:S(2)}) collective-permute-start(bf16[128,12,64]{0,2,1:T(8,128)(2,1)S(1)} %copy.120), channel_id=1, source_target_pairs={{0,2},{2,4},{4,6},{6,8},{8,10},{10,12},{12,14},{14,16},{16,18},{18... | collective-permute-start | bytes 589832 | tf_op jit(solution)/shard_map/while/body/eval_jaxpr/ppermute | solution.py:19
  329.1 17.7 %collective-permute-start.6 = (bf16[128,12,64]{0,2,1:T(8,128)(2,1)S(1)}, bf16[128,12,64]{0,2,1:T(8,128)(2,1)}, u32[]{:S(2)}, u32[]{:S(2)}) collective-permute-start(bf16[128,12,64]{0,2,1:T(8,128)(2,1)S(1)} %copy.121), channel_id=1, source_target_pairs={{0,2},{2,4},{4,6},{6,8},{8,10},{10,12},{12,14},{14,16},{16,18},{18... | collective-permute-start | bytes 589832 | tf_op jit(solution)/shard_map/while/body/eval_jaxpr/ppermute | solution.py:19
  347.7 18.6 %collective-permute-start.5 = (bf16[128,12,64]{0,2,1:T(8,128)(2,1)S(1)}, bf16[128,12,64]{0,2,1:T(8,128)(2,1)}, u32[]{:S(2)}, u32[]{:S(2)}) collective-permute-start(bf16[128,12,64]{0,2,1:T(8,128)(2,1)S(1)} %copy.120), channel_id=1, source_target_pairs={{0,2},{2,4},{4,6},{6,8},{8,10},{10,12},{12,14},{14,16},{16,18},{18... | collective-permute-start | bytes 589832 | tf_op jit(solution)/shard_map/while/body/eval_jaxpr/ppermute | solution.py:19
  348.7 17.7 %collective-permute-start.6 = (bf16[128,12,64]{0,2,1:T(8,128)(2,1)S(1)}, bf16[128,12,64]{0,2,1:T(8,128)(2,1)}, u32[]{:S(2)}, u32[]{:S(2)}) collective-permute-start(bf16[128,12,64]{0,2,1:T(8,128)(2,1)S(1)} %copy.121), channel_id=1, source_target_pairs={{0,2},{2,4},{4,6},{6,8},{8,10},{10,12},{12,14},{14,16},{16,18},{18... | collective-permute-start | bytes 589832 | tf_op jit(solution)/shard_map/while/body/eval_jaxpr/ppermute | solution.py:19
  367.3 18.5 %collective-permute-start.5 = (bf16[128,12,64]{0,2,1:T(8,128)(2,1)S(1)}, bf16[128,12,64]{0,2,1:T(8,128)(2,1)}, u32[]{:S(2)}, u32[]{:S(2)}) collective-permute-start(bf16[128,12,64]{0,2,1:T(8,128)(2,1)S(1)} %copy.120), channel_id=1, source_target_pairs={{0,2},{2,4},{4,6},{6,8},{8,10},{10,12},{12,14},{14,16},{16,18},{18... | collective-permute-start | bytes 589832 | tf_op jit(solution)/shard_map/while/body/eval_jaxpr/ppermute | solution.py:19
  368.3 17.5 %collective-permute-start.6 = (bf16[128,12,64]{0,2,1:T(8,128)(2,1)S(1)}, bf16[128,12,64]{0,2,1:T(8,128)(2,1)}, u32[]{:S(2)}, u32[]{:S(2)}) collective-permute-start(bf16[128,12,64]{0,2,1:T(8,128)(2,1)S(1)} %copy.121), channel_id=1, source_target_pairs={{0,2},{2,4},{4,6},{6,8},{8,10},{10,12},{12,14},{14,16},{16,18},{18... | collective-permute-start | bytes 589832 | tf_op jit(solution)/shard_map/while/body/eval_jaxpr/ppermute | solution.py:19
  401.0 20.1 %collective-permute-start.12 = (bf16[128,12,64]{0,2,1:T(8,128)(2,1)S(1)}, bf16[128,12,64]{0,2,1:T(8,128)(2,1)S(1)}, u32[]{:S(2)}, u32[]{:S(2)}) collective-permute-start(bf16[128,12,64]{0,2,1:T(8,128)(2,1)S(1)} %add_convert_fusion), channel_id=1, source_target_pairs={{0,24},{2,26},{4,28},{6,30},{8,0},{10,2},{12,4},{14,6},{16,8},{18,... | collective-permute-start | bytes 589832 | tf_op jit(solution)/shard_map/ppermute | solution.py:19
  457.2 885.4 %all-gather.24.cloned.1.call-start = ((), (), s32[]{:S(2)}) async-start(), calls=%async_computation.4 | async-start | bytes 15066624 | tf_op jit(solution)/shard_map/all_gather | solution.py:288
  (120 other events, 1785.9 us)
Sparse Core Ops, SparseCore 0:
  9.7 52.3 all-gather.15
  63.6 22.7 all-gather.17
  87.9 62.6 all-gather.19
  151.9 62.6 all-gather.21
  457.3 319.5 all-reduce.4
  1227.4 115.1 all-gather.23
where the time goes:
time: 1590 us; the launch traced here: 1580 us
  waiting for transfers between devices  608 us (38%)
  blocking collectives  337 us (21%)
  other arithmetic  326 us (21%)
  local copies, waits for them, and re-layouts  183 us (12%)
  matrix products  79.7 us (5%)
  starting transfers between devices  28.9 us (2%)
    unnamed x7, waiting for transfers between devices  320 us
    unnamed x1, blocking collectives  298 us
    convert_element_type x1, other arithmetic, body(): summed_flat = lax.all_gather(own_part.astype(jnp.bfloat16), 'ctx', axis=0...  153 us
    another operation x1, other arithmetic, body(): spread_shard = spread_shard.reshape(ctx_count, piece_len)  130 us
    ppermute x69, waiting for transfers between devices, passed_along(): lax.ppermute(value, axis, [(i, (i + by) % length) for i in range(length)])  118 us
    all_gather x1, waiting for transfers between devices, body(): lax.all_gather(own_part.astype(jnp.bfloat16), 'ctx', axis=0, tiled=True)  112 us
    unnamed x150, local copies, waits for them, and re-layouts  51.5 us
    all_gather x1, waiting for transfers between devices, body(): lax.all_gather(w_back, 'wsh', axis=0, tiled=True)  47.7 us
  transfers between devices with their start and end apart: 75, of which 28 were waited for; matrix products, arithmetic and copies ran while one was open for 8% of the time, Pallas kernels for 0%

commit v1 on v0

v1 whole, which is shorter than its diff:
```python
import functools
import types

import jax
import jax.numpy as jnp
from jax import lax
from jax.experimental import pallas as pl
from jax.experimental.pallas import tpu as pltpu
from jax.sharding import PartitionSpec as P

HEAD_DIM = 64
GROUP = 4
GROUP_HEADS = 3
BLOCK = 128
PLANE = GROUP * BLOCK
MODEL = 768
FF = 3072
HALF = MODEL // 2
LANES = GROUP_HEADS * HEAD_DIM
TILES = 4
OWN_ROWS = (4 * 2 * BLOCK, 0)
BOTH = 2 * BLOCK
EPSILON = 1e-05
NEGATIVE = -1e30
ROOT_HALF = 0.7071067811865476
INV_ROOT_TAU = 0.3989422804014327
SCALE = HEAD_DIM**-0.5
MESH = pl.DeviceIdType.MESH
F32 = jnp.float32
BF16 = jnp.bfloat16
NT = (((1,), (1,)), ((), ()))
TN = (((0,), (0,)), ((), ()))


class Place:
    def __init__(self, planes):
        self.n = planes
        self.c = lax.axis_index("ctx")
        self.x = lax.axis_index("wsh")
        self.p = self.c // GROUP
        self.r = self.c % GROUP
        self.y = self.r // 2
        self.k = self.r % 2
        self.parity = self.p % 2
        self.sister = (self.c + 1 - 2 * self.k, self.x)
        self.beside = (self.c + 2 - 4 * self.y, self.x)
        self.across = (self.c, 1 - self.x)
        self.pair = (self.c + GROUP * (1 - 2 * self.parity), self.x)
        self.up = (self.c + GROUP, self.x)
        self.down = (self.c - GROUP, self.x)
        self.has_up = self.p < planes - 1
        self.has_down = self.p > 0

    def peer(self, d):
        if d == 1:
            return self.y * 2 + (1 - self.k)
        if d == 2:
            return (1 - self.y) * 2 + self.k
        return (1 - self.y) * 2 + (1 - self.k)

    def in_plane(self, position):
        return (self.p * GROUP + position, self.x)

    def plane(self, p):
        return (p * GROUP + self.r, self.x)


def signal(sem, device):
    pl.semaphore_signal(sem, inc=1, device_id=device, device_id_type=MESH)


def greet(at):
    barrier = pltpu.get_barrier_semaphore()
    for d in (1, 2, 3):
        signal(barrier, at.in_plane(at.peer(d)))
    signal(barrier, at.across)

    def other_plane(d, carry):
        signal(barrier, at.plane((at.p + d) % at.n))
        return carry

    lax.fori_loop(1, at.n, other_plane, 0)
    pl.semaphore_wait(barrier, 4 + at.n - 1)


def remote(src, dst, sems, index, device, recv_index=None):
    send, recv = sems
    return pltpu.make_async_remote_copy(
        src_ref=src,
        dst_ref=dst,
        send_sem=send.at[index],
        recv_sem=recv.at[index if recv_index is None else recv_index],
        device_id=device,
        device_id_type=MESH,
    )


def lane_head(shape, first):
    return lax.broadcasted_iota(jnp.int32, shape, 1) // HEAD_DIM - first


def column_of(row):
    return jnp.broadcast_to(row, (BLOCK, BLOCK)).T


def chunk_of(rows, planes):
    chunk = -(-(-(-rows // planes)) // 16) * 16
    while rows % chunk:
        chunk += 16
    return chunk


SET_ROWS = (HALF, 512, HALF)
SET_WIDTH = (MODEL, MODEL, 640)
QUARTER = HALF // GROUP


def scratch_plan(planes):
    steps = planes.bit_length() - 1
    buffers = dict(
        wq=((MODEL, 3 * MODEL), BF16),
        wo=((MODEL, MODEL), BF16),
        wi=((MODEL, FF), BF16),
        wb=((FF, MODEL), BF16),
        bias_own=((16, HALF), BF16),
        bias2=((2, 16, HALF), BF16),
        dout_far=((BLOCK, MODEL), BF16),
        ids=((3, GROUP, 8, BLOCK), F32),
        acc=((BLOCK, 3 * MODEL), F32),
        qsend=((GROUP, BLOCK, 256), BF16),
        kvsend=((GROUP, BLOCK, 2 * LANES), BF16),
        qp=((PLANE, 256), BF16),
        kv=((3 * PLANE, 2 * LANES), BF16),
        og=((PLANE, 256), F32),
        lse=((PLANE, BLOCK), F32),
        asend=((GROUP, BLOCK, 256), BF16),
        arecv=((GROUP, BLOCK, 256), BF16),
        tok_plane=((PLANE, MODEL), BF16),
        tok2=((BOTH, MODEL), BF16),
        att2=((BOTH, MODEL), BF16),
        unit_one=((BOTH, MODEL), F32),
        norm_low=((BOTH, MODEL), BF16),
        act=((BOTH, FF), BF16),
        d_inner=((BOTH, FF), BF16),
        d_second=((BOTH, MODEL), BF16),
        d_first=((BOTH, MODEL), BF16),
        second=((BOTH, MODEL), F32),
        slope=((4 * BOTH + HALF, MODEL), F32),
        out_tile=((HALF, MODEL), F32),
        dsend=((GROUP, BLOCK, 256), BF16),
        do=((PLANE, 256), BF16),
        grads=((3 * PLANE, 2 * LANES), F32),
        dq=((PLANE, 256), F32),
        k_ids=((3 * PLANE, BLOCK), F32),
        stats=((2 * GROUP_HEADS, 8, PLANE), F32),
        halo_send=((2, PLANE, 2 * LANES), BF16),
        halo=((2, PLANE, 2 * LANES), BF16),
        d_group=((PLANE, 640), BF16),
        d_recv=((GROUP, BLOCK, 640), BF16),
        d_packed=((BLOCK, 3 * MODEL), BF16),
        q_sum=((HALF, 640), F32),
        x_send=((HALF, 640), BF16),
        x_recv=((HALF, 640), BF16),
        small_recv=((2 + steps, 24, MODEL), F32),
        line_send=((8, 640), F32),
        line_recv=((8, 640), F32),
    )
    for g, (rows, width) in enumerate(zip(SET_ROWS, SET_WIDTH)):
        chunk = chunk_of(rows, planes)
        if g < 2:
            buffers[f"core_send{g}"] = ((2, rows, width), BF16)
            buffers[f"core_recv{g}"] = ((2, rows, width), BF16)
            buffers[f"y_send{g}"] = ((rows, width), BF16)
            buffers[f"y_recv{g}"] = ((rows, width), BF16)
        buffers[f"z_send{g}"] = ((rows, width), BF16)
        buffers[f"z_recv{g}"] = ((planes, chunk, width), BF16)
        buffers[f"final{g}"] = ((chunk, width), BF16)
    semaphores = dict(
        local=(4 + 3,),
        wx=(4, 2),
        wy=(4, 2),
        wz=(4, 2),
        wc=(4, 5),
        ex=(5,),
        tp=(4,),
        a2a=(6, 4),
        halo_f=(2, 5),
        halo_b=(2,),
        core=(4,),
        xs=(planes,),
        ys=(2, planes),
        zs=(3, planes),
        gu=(3, planes),
        gd=(3, planes),
        gy=(3, planes),
        gc=(3, planes),
        gf=(3, planes),
        sm=(2 + steps,),
    )
    return buffers, semaphores


ARGS = ["tokens", "doc_ids", "w_qkv", "b_query", "b_value", "w_out", "b_out", "ln1_gain"]
ARGS += ["ln1_bias", "w_in", "b_in", "w_back", "b_back", "ln2_gain", "ln2_bias", "d_out"]
RESULTS = ["result", "d_tokens", "sums0", "sums1", "sums2", "small"]


def layer_kernel(planes, names, sem_names, *refs):
    split = len(ARGS) + len(RESULTS) + len(names)
    b = types.SimpleNamespace(**dict(zip(ARGS + RESULTS + names, refs[:split])))
    pairs = refs[split:]
    s = types.SimpleNamespace(
        **{n: (pairs[2 * i], pairs[2 * i + 1]) for i, n in enumerate(sem_names)}
    )
    at = Place(planes)
    sent = []

    def start(copy):
        copy.start()
        sent.append(copy)

    def block_rows(first, i):
        return pl.ds(pl.multiple_of(first + i * BLOCK, BLOCK), BLOCK)

    b.ids[1, at.r] = jnp.broadcast_to(b.doc_ids[...].astype(F32), (8, BLOCK))

    @pl.when(jnp.logical_not(at.has_down))
    def _():
        b.kv[pl.ds(0, PLANE), :] = jnp.zeros((PLANE, 2 * LANES), BF16)
        b.ids[0] = jnp.full((GROUP, 8, BLOCK), -1.0, F32)

    @pl.when(jnp.logical_not(at.has_up))
    def _():
        b.kv[pl.ds(2 * PLANE, PLANE), :] = jnp.zeros((PLANE, 2 * LANES), BF16)
        b.ids[2] = jnp.full((GROUP, 8, BLOCK), -1.0, F32)

    vectors = [b.b_query, b.b_value, b.b_out, b.ln1_gain, b.ln1_bias]
    lines = [v[...].astype(F32).reshape(1, HALF) for v in vectors]
    lines += [
        b.b_in[pl.ds(i * HALF, HALF)].astype(F32).reshape(1, HALF) for i in range(4)
    ]
    lines += [
        v[...].astype(F32).reshape(1, HALF) for v in (b.b_back, b.ln2_gain, b.ln2_bias)
    ]
    lines.append(jnp.zeros((4, HALF), F32))
    packed_bias = jnp.concatenate(lines, axis=0).astype(BF16)
    b.bias_own[...] = packed_bias
    b.bias2[at.x] = packed_bias
    greet(at)

    shards = (b.w_qkv, b.w_out, b.w_in, b.w_back)
    wholes = (b.wq, b.wo, b.wi, b.wb)
    direct = (True, True, False, False)
    own_q = at.y * 2 + at.parity
    diag_q = (1 - at.y) * 2 + (1 - at.parity)
    beside_q = (1 - at.y) * 2 + at.parity
    pair_q = at.y * 2 + (1 - at.parity)

    def rows(w, quarter, core):
        eighth = shards[w].shape[0] // 8
        return pl.multiple_of((quarter * 2 + core) * eighth, 16), eighth

    def far(w, quarter, core, part=None):
        first, size = rows(w, quarter, core)
        base = (1 - at.x) * shards[w].shape[0]
        lines = pl.ds(pl.multiple_of(base + first, 16), size)
        if part is None:
            return wholes[w].at[lines]
        width = shards[w].shape[1] // 2
        return wholes[w].at[lines, pl.ds(part * width, width)]

    def across_copy(w, i):
        first, size = rows(w, (own_q, diag_q)[i], at.k)
        base = at.x * shards[w].shape[0]
        return remote(
            shards[w].at[pl.ds(first, size)],
            wholes[w].at[pl.ds(pl.multiple_of(base + first, 16), size)],
            s.wx,
            (w, i),
            at.across,
        )

    def piece_copy(w, quarter, sems, index, device, part=None, core=None):
        piece = far(w, quarter, at.k if core is None else core, part)
        return remote(piece, piece, sems, (w, index), device)

    def relay_own(w):
        piece_copy(w, own_q, s.wx, 0, at.across).wait_recv()
        start(piece_copy(w, own_q, s.wy, 0, at.beside))
        start(piece_copy(w, own_q, s.wz, 0, at.pair))
        start(piece_copy(w, own_q, s.wc, 0, at.sister))

    def relay_rest(w):
        if direct[w]:
            piece_copy(w, diag_q, s.wx, 1, at.across).wait_recv()
            start(piece_copy(w, diag_q, s.wc, 1, at.sister))
        piece_copy(w, beside_q, s.wy, 0, at.beside).wait_recv()
        if not direct[w]:
            start(piece_copy(w, beside_q, s.wz, 1, at.pair, part=1))
        start(piece_copy(w, beside_q, s.wc, 2, at.sister))
        piece_copy(w, pair_q, s.wz, 0, at.pair).wait_recv()
        if not direct[w]:
            start(piece_copy(w, pair_q, s.wy, 1, at.beside, part=0))
        start(piece_copy(w, pair_q, s.wc, 3, at.sister))

    def relay_diagonal(w):
        piece_copy(w, diag_q, s.wy, 1, at.beside, part=0).wait_recv()
        start(piece_copy(w, diag_q, s.wc, 1, at.sister, part=0))
        piece_copy(w, diag_q, s.wz, 1, at.pair, part=1).wait_recv()
        start(piece_copy(w, diag_q, s.wc, 4, at.sister, part=1))

    def sister_arrivals(w):
        other = 1 - at.k
        piece_copy(w, own_q, s.wc, 0, at.sister, core=other).wait_recv()
        piece_copy(w, beside_q, s.wc, 2, at.sister, core=other).wait_recv()
        piece_copy(w, pair_q, s.wc, 3, at.sister, core=other).wait_recv()
        if direct[w]:
            piece_copy(w, diag_q, s.wc, 1, at.sister, core=other).wait_recv()
        else:
            piece_copy(w, diag_q, s.wc, 1, at.sister, part=0, core=other).wait_recv()
            piece_copy(w, diag_q, s.wc, 4, at.sister, part=1, core=other).wait_recv()

    near_tokens = pl.ds(0, BLOCK)
    far_tokens = pl.ds(BLOCK, BLOCK)
    bias_copy = remote(b.bias_own, b.bias2.at[at.x], s.ex, 0, at.across)
    tok_copy = remote(b.tokens.at[0], b.tok2.at[far_tokens], s.ex, 1, at.across)
    dout_copy = remote(b.d_out.at[0], b.dout_far, s.ex, 2, at.across)
    for i in range(2):
        start(across_copy(0, i))
    start(bias_copy)
    for d in (1, 2, 3):
        mine = b.ids.at[1, at.r]
        start(remote(mine, mine, s.a2a, (0, d), at.in_plane(at.peer(d))))
    own_copies = []
    for w in range(4):
        size = shards[w].shape[0]
        own_copies.append(
            pltpu.make_async_copy(
                shards[w],
                wholes[w].at[pl.ds(pl.multiple_of(at.x * size, 16), size)],
                s.local[0].at[w],
            )
        )
    own_copies[0].start()

    near_rows = pl.multiple_of(at.x * HALF, HALF)
    far_rows = pl.multiple_of((1 - at.x) * HALF, HALF)
    b.tok2[near_tokens, :] = b.tokens[0]
    b.tok_plane[block_rows(0, at.r), :] = b.tokens[0]
    own_copies[0].wait()
    near = b.tokens[0, :, pl.ds(near_rows, HALF)]
    for j in range(3):
        cols = slice(j * MODEL, (j + 1) * MODEL)
        b.acc[:, cols] = jnp.dot(
            near, b.wq[pl.ds(near_rows, HALF), cols], preferred_element_type=F32
        )
    for w in (1, 2, 3):
        own_copies[w].start()
    relay_own(0)
    relay_rest(0)
    for i in range(2):
        start(across_copy(1, i))
    start(across_copy(2, 0))
    remote(b.bias_own, b.bias2.at[1 - at.x], s.ex, 0, at.across).wait_recv()
    halves = (b.bias2[0].astype(F32), b.bias2[1].astype(F32))
    bias = jnp.concatenate(halves, axis=1)
    sister_arrivals(0)
    apart = b.tokens[0, :, pl.ds(far_rows, HALF)]
    for j in range(3):
        cols = slice(j * MODEL, (j + 1) * MODEL)
        part = b.acc[:, cols] + jnp.dot(
            apart, b.wq[pl.ds(far_rows, HALF), cols], preferred_element_type=F32
        )
        if j == 0:
            part = part + bias[0:1]
        if j == 2:
            part = part + bias[1:2]
        b.acc[:, cols] = part

    zero_lanes = jnp.zeros((BLOCK, HEAD_DIM), F32)
    for g in range(GROUP):
        cols = [
            b.acc[:, j * MODEL + g * LANES : j * MODEL + (g + 1) * LANES] for j in range(3)
        ]
        b.qsend[g] = jnp.concatenate([cols[0], zero_lanes], axis=1).astype(BF16)
        b.kvsend[g] = jnp.concatenate([cols[1], cols[2]], axis=1).astype(BF16)

    for d in (1, 2, 3):
        g = at.peer(d)
        start(
            remote(
                b.kvsend.at[g],
                b.kv.at[block_rows(PLANE, at.r)],
                s.a2a,
                (1, d),
                at.in_plane(g),
            )
        )
    for d in (1, 2, 3):
        g = at.peer(d)
        start(
            remote(
                b.qsend.at[g], b.qp.at[block_rows(0, at.r)], s.a2a, (2, d), at.in_plane(g)
            )
        )
    b.kv[block_rows(PLANE, at.r), :] = b.kvsend[at.r]
    b.qp[block_rows(0, at.r), :] = b.qsend[at.r]

    def both_ways(up, down, act):
        @pl.when(at.has_up)
        def _():
            act(up)

        @pl.when(at.has_down)
        def _():
            act(down)

    def go(copy):
        copy.start()

    def block_of(d):
        return at.r if d == 0 else at.peer(d)

    def up_kv(d):
        i = block_of(d)
        return remote(
            b.kv.at[block_rows(PLANE, i)], b.kv.at[block_rows(0, i)], s.halo_f, (0, d), at.up
        )

    def down_kv(d):
        i = block_of(d)
        return remote(
            b.kv.at[block_rows(PLANE, i)],
            b.kv.at[block_rows(2 * PLANE, i)],
            s.halo_f,
            (1, d),
            at.down,
        )

    up_ids = remote(b.ids.at[1], b.ids.at[0], s.halo_f, (0, 4), at.up)
    down_ids = remote(b.ids.at[1], b.ids.at[2], s.halo_f, (1, 4), at.down)

    def from_peer(piece, kind, d):
        remote(piece, piece, s.a2a, (kind, d), at.in_plane(at.peer(d))).wait_recv()

    both_ways(up_kv(0), down_kv(0), go)
    for d in (1, 2, 3):
        from_peer(b.ids.at[1, at.peer(d)], 0, d)
    both_ways(up_ids, down_ids, go)
    relay_own(1)
    for d in (1, 2, 3):
        from_peer(b.kv.at[block_rows(PLANE, at.peer(d))], 1, d)
        both_ways(up_kv(d), down_kv(d), go)
    relay_rest(1)
    relay_own(2)
    start(across_copy(3, 0))
    start(tok_copy)
    for d in (1, 2, 3):
        from_peer(b.qp.at[block_rows(0, at.peer(d))], 2, d)
    relay_rest(2)

    @pl.when(at.has_down)
    def _():
        for d in range(4):
            piece = b.kv.at[block_rows(0, block_of(d))]
            remote(piece, piece, s.halo_f, (0, d), at.down).wait_recv()
        remote(b.ids.at[0], b.ids.at[0], s.halo_f, (0, 4), at.down).wait_recv()

    @pl.when(at.has_up)
    def _():
        for d in range(4):
            piece = b.kv.at[block_rows(2 * PLANE, block_of(d))]
            remote(piece, piece, s.halo_f, (1, d), at.up).wait_recv()
        remote(b.ids.at[2], b.ids.at[2], s.halo_f, (1, 4), at.up).wait_recv()

    def attend(t, carry):
        q_rows = block_rows(0, t)
        q_ids = column_of(b.ids[1, t][0:1, :])[:, 0:1]
        k_ids = jnp.concatenate(
            [b.ids[i, j][0:1, :] for i in range(3) for j in range(GROUP)], axis=1
        )
        same = q_ids == k_ids
        total = jnp.zeros((BLOCK, 256), F32)
        logs = jnp.zeros((BLOCK, BLOCK), F32)
        for h in range(GROUP_HEADS):
            q = b.qp[q_rows, :] * SCALE
            q = jnp.where(lane_head((BLOCK, 256), 0) == h, q, jnp.zeros_like(q))
            score = lax.dot_general(q, b.kv[:, 0:256], NT, preferred_element_type=F32)
            score = jnp.where(same, score, NEGATIVE)
            peak = jnp.max(score, axis=1, keepdims=True)
            weight = jnp.exp(score - peak)
            summed = jnp.sum(weight, axis=1, keepdims=True)
            out = jnp.dot(weight.astype(BF16), b.kv[:, 128:384], preferred_element_type=F32)
            out = out / summed
            total = jnp.where(lane_head((BLOCK, 256), 1) == h, out, total)
            lane = lax.broadcasted_iota(jnp.int32, (BLOCK, BLOCK), 1)
            logs = jnp.where(lane == h, peak + jnp.log(summed), logs)
        b.og[q_rows, :] = total
        b.lse[q_rows, :] = logs
        b.asend[t] = total.astype(BF16)
        return carry

    lax.fori_loop(0, GROUP, attend, 0)

    for d in (1, 2, 3):
        i = at.peer(d)
        start(remote(b.asend.at[i], b.arecv.at[at.r], s.a2a, (3, d), at.in_plane(i)))
    b.arecv[at.r] = b.asend[at.r]
    relay_own(3)
    for d in (1, 2, 3):
        from_peer(b.arecv.at[at.peer(d)], 3, d)
    b.att2[near_tokens, :] = jnp.concatenate(
        [b.arecv[g].astype(F32)[:, HEAD_DIM : HEAD_DIM + LANES] for g in range(GROUP)], axis=1
    ).astype(BF16)
    att_copy = remote(b.att2.at[near_tokens], b.att2.at[far_tokens], s.ex, 3, at.across)
    start(att_copy)
    start(dout_copy)
    relay_rest(3)
    relay_diagonal(2)
    own_copies[1].wait()
    sister_arrivals(1)
    tok_copy.wait_recv()
    att_copy.wait_recv()

    def normalise(hidden):
        center = hidden - jnp.mean(hidden, -1, keepdims=True)
        inverse = lax.rsqrt(jnp.mean(center * center, -1, keepdims=True) + EPSILON)
        return center * inverse, inverse

    def norm_back(upstream, unit, inverse, gain):
        scaled = upstream * gain
        return inverse * (
            scaled
            - jnp.mean(scaled, -1, keepdims=True)
            - unit * jnp.mean(scaled * unit, -1, keepdims=True)
        )

    def column_sum(value):
        return jnp.sum(value, axis=0, keepdims=True)

    def tok_block(i, sem, device):
        piece = b.tok_plane.at[block_rows(0, i)]
        return remote(piece, piece, s.tp, sem, device)

    start(tok_block(at.r, 0, at.beside))
    start(tok_block(at.r, 1, at.sister))
    first = (
        b.tok2[...].astype(F32)
        + jnp.dot(b.att2[...], b.wo[...], preferred_element_type=F32)
        + bias[2:3]
    )
    unit_one, inverse_one = normalise(first)
    b.unit_one[...] = unit_one
    normed = unit_one * bias[3:4] + bias[4:5]
    b.norm_low[...] = normed.astype(BF16)
    b.second[...] = normed + bias[9:10]
    relay_diagonal(3)
    for w in (2, 3):
        own_copies[w].wait()
        sister_arrivals(w)
    for c in range(4):
        cols = slice(c * MODEL, (c + 1) * MODEL)
        part = halves[c // 2]
        i = 5 + 2 * (c % 2)
        line = jnp.concatenate([part[i : i + 1], part[i + 1 : i + 2]], axis=1)
        inner = jnp.dot(b.norm_low[...], b.wi[:, cols], preferred_element_type=F32) + line
        gate = 0.5 * (1.0 + lax.erf(inner * ROOT_HALF))
        activation = (inner * gate).astype(BF16)
        b.act[:, cols] = activation
        b.slope[c * BOTH : (c + 1) * BOTH, :] = (
            gate + inner * jnp.exp(-0.5 * inner * inner) * INV_ROOT_TAU
        )
        b.second[...] += jnp.dot(activation, b.wb[cols, :], preferred_element_type=F32)
    unit_two, inverse_two = normalise(b.second[...])
    b.result[...] = (unit_two[:BLOCK] * bias[10:11] + bias[11:12]).astype(BF16)
    dout_copy.wait_recv()
    upstream = jnp.concatenate([b.d_out[0], b.dout_far[...]], axis=0).astype(F32)
    b.small[...] = jnp.zeros_like(b.small)
    b.small[10:11, :] = column_sum(upstream * unit_two)
    b.small[11:12, :] = column_sum(upstream)
    d_second = norm_back(upstream, unit_two, inverse_two, bias[10:11])
    b.small[9:10, :] = column_sum(d_second)
    b.d_second[...] = d_second.astype(BF16)
    b.second[...] = d_second

    chunks = [chunk_of(rows, planes) for rows in SET_ROWS]
    owners = [rows // chunk for rows, chunk in zip(SET_ROWS, chunks)]

    def of(name, group):
        return getattr(b, f"{name}{group}")

    def tile(group, t):
        if group == 0:
            lanes = pl.multiple_of(at.x * (TILES * HALF) + t * HALF, 128)
            left, right = b.act[:, pl.ds(lanes, HALF)], b.d_second[...]
        else:
            left = b.norm_low[:, pl.ds(near_rows, HALF)]
            right = b.d_inner[:, pl.ds(pl.multiple_of(t * MODEL, 128), MODEL)]
        return lax.dot_general(left, right, TN, preferred_element_type=F32)

    def out_quarter(t):
        return b.out_tile[pl.ds(pl.multiple_of(t * QUARTER, 16), QUARTER), :]

    def chunk_rows(group, j):
        return pl.ds(pl.multiple_of(j * chunks[group], 16), chunks[group])

    def own_chunk(group, j):
        if group == 2:
            return b.q_sum.at[chunk_rows(2, j)]
        first_row = OWN_ROWS[group] + j * chunks[group]
        return b.slope.at[pl.ds(pl.multiple_of(first_row, 16), chunks[group])]

    def core_copy(group, i):
        return remote(
            of("core_send", group).at[i],
            of("core_recv", group).at[i],
            s.core,
            group * 2 + i,
            at.sister,
        )

    def y_copy(group, j):
        lines = chunk_rows(group, j)
        return remote(
            of("y_send", group).at[lines],
            of("y_recv", group).at[lines],
            s.ys,
            (group, j),
            at.beside,
        )

    def z_copy(group, j):
        return remote(
            of("z_send", group).at[chunk_rows(group, j)],
            of("z_recv", group).at[at.p],
            s.zs,
            (group, j),
            at.plane(j),
            (group, at.p),
        )

    def each_owner(group, act, first=1):
        def one(d, carry):
            j = (at.p + d) % planes

            @pl.when(j < owners[group])
            def _():
                act(j)

            return carry

        lax.fori_loop(first, first + planes, one, 0)

    def produce(group):
        base = OWN_ROWS[group]
        for i, t in enumerate((at.peer(3), at.peer(1))):
            of("core_send", group)[i, 0:HALF, :] = tile(group, t).astype(BF16)
            if group == 1:
                of("core_send", group)[i, HALF : HALF + QUARTER, :] = out_quarter(t).astype(BF16)
            start(core_copy(group, i))
        passing = tile(group, at.peer(2))
        b.slope[base : base + HALF, :] = tile(group, at.r)
        if group == 1:
            b.slope[base + HALF : base + HALF + QUARTER, :] = out_quarter(at.r)
        core_copy(group, 0).wait_recv()
        come = of("core_recv", group)
        of("y_send", group)[0:HALF, :] = (passing + come[0, 0:HALF, :].astype(F32)).astype(BF16)
        if group == 1:
            lines = slice(HALF, HALF + QUARTER)
            b.y_send1[HALF + QUARTER :, :] = jnp.zeros((BLOCK - QUARTER, MODEL), BF16)
            of("y_send", group)[lines, :] = (
                out_quarter(at.peer(2)) + come[0, lines, :].astype(F32)
            ).astype(BF16)
        each_owner(group, lambda j: y_copy(group, j).start())
        core_copy(group, 1).wait_recv()
        used = SET_ROWS[0] if group == 0 else HALF + QUARTER
        b.slope[base : base + used, :] += come[1, 0:used, :].astype(F32)

    def scatter(group):
        def act(j):
            mine = own_chunk(group, j)
            if group == 2:
                x_copy(j).wait_recv()
                came = b.x_recv[chunk_rows(2, j), :]
            else:
                y_copy(group, j).wait_recv()
                came = of("y_recv", group)[chunk_rows(group, j), :]
            total = mine[...] + came.astype(F32)
            mine[...] = total

            @pl.when(j != at.p)
            def _():
                of("z_send", group)[chunk_rows(group, j), :] = total.astype(BF16)
                z_copy(group, j).start()

        each_owner(group, act)

    def x_copy(j):
        lines = chunk_rows(2, j)
        return remote(b.x_send.at[lines], b.x_recv.at[lines], s.xs, j, at.across)

    def place(group, t, j):
        first_row = t * SET_ROWS[group] + j * chunks[group]
        return of("sums", group).at[pl.ds(pl.multiple_of(first_row, 16), chunks[group])]

    def gather_copy(group, t, j, sems, device, source=None):
        piece = place(group, t, j)
        return remote(piece if source is None else source, piece, sems, (group, j), device)

    def spread(group, j, source=None):
        @pl.when(jnp.logical_and(j <= at.p, at.has_up))
        def _():
            gather_copy(group, at.r, j, s.gu, at.up, source).start()

        @pl.when(jnp.logical_and(j >= at.p, at.has_down))
        def _():
            gather_copy(group, at.r, j, s.gd, at.down, source).start()

        gather_copy(group, at.r, j, s.gy, at.beside, source).start()
        gather_copy(group, at.r, j, s.gc, at.sister, source).start()

    def settle_copy(group):
        return pltpu.make_async_copy(
            of("final", group), place(group, at.r, at.p), s.local[0].at[4 + group]
        )

    def settle(group):
        @pl.when(at.p < owners[group])
        def _():
            came = of("z_recv", group)

            def add(d, total):
                q = (at.p + d) % planes
                remote(came.at[q], came.at[q], s.zs, (group, q), at.plane(q)).wait_recv()
                return total + came[q].astype(F32)

            total = lax.fori_loop(1, planes, add, own_chunk(group, at.p)[...])
            of("final", group)[...] = total.astype(BF16)
            spread(group, at.p, of("final", group))
            settle_copy(group).start()

    def come_in(group):
        def one(d, carry):
            @pl.when(jnp.logical_and(at.p - d >= 0, at.p - d < owners[group]))
            def _():
                gather_copy(group, at.r, at.p - d, s.gu, at.down).wait_recv()
                spread(group, at.p - d)

            @pl.when(at.p + d < owners[group])
            def _():
                gather_copy(group, at.r, at.p + d, s.gd, at.up).wait_recv()
                spread(group, at.p + d)

            return carry

        lax.fori_loop(1, planes, one, 0)

    def hand_over(group):
        def act(j):
            gather_copy(group, at.peer(2), j, s.gy, at.beside).wait_recv()
            gather_copy(group, at.peer(2), j, s.gf, at.sister).start()

        each_owner(group, act, 0)

    for c in range(4):
        cols = slice(c * MODEL, (c + 1) * MODEL)
        d_inner = (
            lax.dot_general(b.d_second[...], b.wb[cols, :], NT, preferred_element_type=F32)
            * b.slope[c * BOTH : (c + 1) * BOTH, :]
        )
        b.small[5 + c : 6 + c, :] = column_sum(d_inner)
        low = d_inner.astype(BF16)
        b.d_inner[:, cols] = low
        b.second[...] += lax.dot_general(low, b.wi[:, cols], NT, preferred_element_type=F32)
    d_normed = b.second[...]
    unit_one = b.unit_one[...]
    b.small[3:4, :] = column_sum(d_normed * unit_one)
    b.small[4:5, :] = column_sum(d_normed)
    d_first = norm_back(d_normed, unit_one, inverse_one, bias[3:4])
    b.small[2:3, :] = column_sum(d_first)
    d_first_low = d_first.astype(BF16)
    b.d_first[...] = d_first_low
    b.d_tokens[...] = d_first[:BLOCK]
    d_attn = lax.dot_general(d_first_low[:BLOCK], b.wo[...], NT, preferred_element_type=F32)
    for g in range(GROUP):
        b.dsend[g] = jnp.concatenate(
            [zero_lanes, d_attn[:, g * LANES : (g + 1) * LANES]], axis=1
        ).astype(BF16)
    for d in (1, 2, 3):
        g = at.peer(d)
        start(
            remote(
                b.dsend.at[g], b.do.at[block_rows(0, at.r)], s.a2a, (4, d), at.in_plane(g)
            )
        )
    b.do[block_rows(0, at.r), :] = b.dsend[at.r]

    tok_block(at.peer(2), 0, at.beside).wait_recv()
    start(tok_block(at.peer(2), 2, at.sister))
    produce(0)

    b.grads[...] = jnp.zeros_like(b.grads)
    b.dq[...] = jnp.zeros_like(b.dq)
    for i in range(3):
        for j in range(GROUP):
            b.k_ids[(i * GROUP + j) * BLOCK : (i * GROUP + j + 1) * BLOCK, :] = column_of(
                b.ids[i, j][0:1, :]
            )
    q_ids = jnp.concatenate([b.ids[1, j][0:1, :] for j in range(GROUP)], axis=1)
    lse_rows = b.lse[...].T
    for d in (1, 2, 3):
        from_peer(b.do.at[block_rows(0, at.peer(d))], 4, d)
    prod = (b.do[...].astype(F32) * b.og[...]).T
    for h in range(GROUP_HEADS):
        b.stats[h] = jnp.broadcast_to(lse_rows[h : h + 1, :], (8, PLANE))
        b.stats[GROUP_HEADS + h] = jnp.broadcast_to(
            column_sum(prod[HEAD_DIM * (h + 1) : HEAD_DIM * (h + 2), :]), (8, PLANE)
        )

    def visit(h, i):
        span = pl.ds(i * PLANE, PLANE)
        pick_q = lane_head((PLANE, 256), 0) == h
        q = b.qp[...]
        q = jnp.where(pick_q, q, jnp.zeros_like(q))
        dout = b.do[...]
        dout = jnp.where(lane_head((PLANE, 256), 1) == h, dout, jnp.zeros_like(dout))
        keys = b.kv[span, 0:256]
        score = lax.dot_general(keys, q * SCALE, NT, preferred_element_type=F32)
        same = b.k_ids[span, 0:1] == q_ids
        prob = jnp.where(same, jnp.exp(score - b.stats[h][0:1, :]), 0.0)
        d_prob = lax.dot_general(b.kv[span, 128:384], dout, NT, preferred_element_type=F32)
        d_score = (prob * (d_prob - b.stats[GROUP_HEADS + h][0:1, :]) * SCALE).astype(BF16)
        b.grads[span, 0:256] += jnp.dot(d_score, q, preferred_element_type=F32)
        b.grads[span, 128:384] += jnp.dot(
            prob.astype(BF16), dout, preferred_element_type=F32
        )
        b.dq[...] += jnp.where(
            pick_q, lax.dot_general(d_score, keys, TN, preferred_element_type=F32), 0.0
        )

    def visit_plane(i):
        def one(h, carry):
            visit(h, i)
            return carry

        lax.fori_loop(0, GROUP_HEADS, one, 0)

    down_grads = remote(b.halo_send.at[0], b.halo.at[1], s.halo_b, 0, at.down)
    up_grads = remote(b.halo_send.at[1], b.halo.at[0], s.halo_b, 1, at.up)
    visit_plane(0)
    b.halo_send[0] = b.grads[pl.ds(0, PLANE), :].astype(BF16)

    @pl.when(at.has_down)
    def _():
        down_grads.start()

    visit_plane(2)
    b.halo_send[1] = b.grads[pl.ds(2 * PLANE, PLANE), :].astype(BF16)

    @pl.when(at.has_up)
    def _():
        up_grads.start()

    visit_plane(1)
    b.d_group[:, 0:256] = b.dq[...].astype(BF16)
    b.out_tile[...] = lax.dot_general(
        b.att2[:, pl.ds(near_rows, HALF)], b.d_first[...], TN, preferred_element_type=F32
    )
    produce(1)

    @pl.when(at.has_up)
    def _():
        remote(b.halo.at[1], b.halo.at[1], s.halo_b, 0, at.up).wait_recv()
        b.grads[pl.ds(PLANE, PLANE), :] += b.halo[1].astype(F32)

    @pl.when(at.has_down)
    def _():
        remote(b.halo.at[0], b.halo.at[0], s.halo_b, 1, at.down).wait_recv()
        b.grads[pl.ds(PLANE, PLANE), :] += b.halo[0].astype(F32)

    b.d_group[:, 256:640] = b.grads[pl.ds(PLANE, PLANE), :].astype(BF16)

    tok_block(at.peer(1), 1, at.sister).wait_recv()
    tok_block(at.peer(3), 2, at.sister).wait_recv()
    b.x_send[...] = lax.dot_general(
        b.tok_plane[:, pl.ds(far_rows, HALF)], b.d_group[...], TN, preferred_element_type=F32
    ).astype(BF16)
    each_owner(2, lambda j: x_copy(j).start())
    b.line_send[...] = jnp.broadcast_to(column_sum(b.d_group[...].astype(F32)), (8, 640))
    line_copy = remote(b.line_send, b.line_recv, s.ex, 4, at.across)
    start(line_copy)
    for d in (1, 2, 3):
        i = at.peer(d)
        start(
            remote(
                b.d_group.at[block_rows(0, i)],
                b.d_recv.at[at.r],
                s.a2a,
                (5, d),
                at.in_plane(i),
            )
        )
    b.d_recv[at.r] = b.d_group[block_rows(0, at.r), :]
    b.q_sum[...] = lax.dot_general(
        b.tok_plane[:, pl.ds(near_rows, HALF)], b.d_group[...], TN, preferred_element_type=F32
    )
    scatter(0)
    scatter(2)

    partners = [at.sister, at.beside]
    span = 1
    while span < planes:
        partners.append((at.c + GROUP * span * (1 - 2 * ((at.p // span) % 2)), at.x))
        span *= 2

    def small_copy(i):
        return remote(b.small, b.small_recv.at[i], s.sm, i, partners[i])

    def small_finish(i):
        small_copy(i).wait()
        b.small[...] += b.small_recv[i]

    line_copy.wait_recv()
    line = b.line_send[...] + b.line_recv[...]
    mine = lax.broadcasted_iota(jnp.int32, (8, 640), 0) == at.r
    b.small[16:24, 0:640] = jnp.where(mine, line, 0.0)
    small_copy(0).start()
    settle(0)
    small_finish(0)
    small_copy(1).start()
    scatter(1)
    small_finish(1)
    small_copy(2).start()
    settle(2)
    come_in(0)
    small_finish(2)
    small_copy(3).start()

    for d in (1, 2, 3):
        from_peer(b.d_recv.at[at.peer(d)], 5, d)
    for j, first_lane in enumerate((0, 256, 448)):
        b.d_packed[:, j * MODEL : (j + 1) * MODEL] = jnp.concatenate(
            [
                b.d_recv[g].astype(F32)[:, first_lane : first_lane + LANES]
                for g in range(GROUP)
            ],
            axis=1,
        ).astype(BF16)
    b.d_tokens[...] += lax.dot_general(
        b.d_packed[...], b.wq[...], NT, preferred_element_type=F32
    )

    hand_over(0)
    small_finish(3)
    for i in range(4, len(partners)):
        small_copy(i).start()
        small_finish(i)
    settle(1)
    come_in(2)
    hand_over(2)
    come_in(1)
    hand_over(1)

    for group in range(3):

        def last(j, carry, group=group):
            gather_copy(group, at.peer(1), j, s.gc, at.sister).wait_recv()
            gather_copy(group, at.peer(3), j, s.gf, at.sister).wait_recv()
            gather_copy(group, at.r, j, s.gy, at.beside).wait_send()
            gather_copy(group, at.r, j, s.gc, at.sister).wait_send()
            gather_copy(group, at.peer(2), j, s.gf, at.sister).wait_send()
            if group == 2:
                x_copy(j).wait_send()
            else:
                y_copy(group, j).wait_send()

            @pl.when(jnp.logical_and(j <= at.p, at.has_up))
            def _():
                gather_copy(group, at.r, j, s.gu, at.up).wait_send()

            @pl.when(jnp.logical_and(j >= at.p, at.has_down))
            def _():
                gather_copy(group, at.r, j, s.gd, at.down).wait_send()

            @pl.when(j != at.p)
            def _():
                z_copy(group, j).wait_send()

            return carry

        lax.fori_loop(0, owners[group], last, 0)

        @pl.when(at.p < owners[group])
        def _(group=group):
            settle_copy(group).wait()

    for copy in sent:
        copy.wait_send()

    def finish(copy):
        copy.wait_send()

    for d in range(4):
        both_ways(up_kv(d), down_kv(d), finish)
    both_ways(up_ids, down_ids, finish)
    both_ways(up_grads, down_grads, finish)


def layer_call(planes, args):
    buffers, semaphores = scratch_plan(planes)
    hbm = pl.BlockSpec(memory_space=pltpu.HBM)
    vmem = pl.BlockSpec(memory_space=pltpu.VMEM)
    weights = ("w_qkv", "w_out", "w_in", "w_back")
    scratch = [pltpu.VMEM(shape, kind) for shape, kind in buffers.values()]
    for shape in semaphores.values():
        scratch += [pltpu.SemaphoreType.DMA(shape)] * 2
    return pl.pallas_call(
        functools.partial(layer_kernel, planes, list(buffers), list(semaphores)),
        out_shape=[
            jax.ShapeDtypeStruct((BLOCK, MODEL), BF16),
            jax.ShapeDtypeStruct((BLOCK, MODEL), F32),
        ]
        + [
            jax.ShapeDtypeStruct((TILES * rows, width), BF16)
            for rows, width in zip(SET_ROWS, SET_WIDTH)
        ]
        + [jax.ShapeDtypeStruct((24, MODEL), F32)],
        in_specs=[hbm if name in weights else vmem for name in ARGS],
        out_specs=[vmem, vmem, hbm, hbm, hbm, vmem],
        scratch_shapes=scratch,
        compiler_params=pltpu.CompilerParams(
            collective_id=0, has_side_effects=True, vmem_limit_bytes=60 * 2**20
        ),
        name="layer",
    )(*args)


def unpack_kernel(result_in, tokens_in, sums0, sums1, sums2, small, *refs):
    result, d_tokens, w_qkv, bq, bv, w_out, bo, g1, o1, w_in, bi, w_back, bb, g2, o2 = refs[:15]
    in0, in1, in2, out_q, out_o, out_i, out_b, come, go = refs[15:]
    loads = []
    for g, (sums, held) in enumerate(((sums0, in0), (sums1, in1), (sums2, in2))):
        for t in range(TILES):
            lines = pl.ds(t * SET_ROWS[g], SET_ROWS[g])
            loads.append(
                pltpu.make_async_copy(sums.at[lines], held.at[t], come.at[g * TILES + t])
            )
    for load in loads:
        load.start()
    stores = [
        pltpu.make_async_copy(result_in, result, go.at[14]),
        pltpu.make_async_copy(tokens_in, d_tokens, go.at[15]),
    ]
    for store in stores:
        store.start()

    def put(source, target, i):
        store = pltpu.make_async_copy(source, target, go.at[i])
        store.start()
        stores.append(store)

    x = lax.axis_index("wsh")
    half = small[0:16, pl.ds(pl.multiple_of(x * HALF, 128), HALF)]
    for ref, row in zip((bo, g1, o1, bb, g2, o2), (2, 3, 4, 9, 10, 11)):
        ref[...] = half[row, :]
    whole = jnp.where(x == 0, small[5:7, :], small[7:9, :])
    bi[pl.ds(0, MODEL)] = whole[0, :]
    bi[pl.ds(MODEL, MODEL)] = whole[1, :]
    for ref, first in ((bq, 0), (bv, 448)):
        row = jnp.concatenate(
            [small[16 + g : 17 + g, first : first + LANES] for g in range(GROUP)], axis=1
        )
        ref[...] = jnp.where(x == 0, row[:, :HALF], row[:, HALF:])[0, :]

    for t in range(TILES):
        loads[t].wait()
        lines = pl.ds(t * HALF, HALF)
        out_b[lines, :] = in0[t].astype(F32)
        put(out_b.at[lines], w_back.at[lines], t)
    for t in range(TILES):
        loads[TILES + t].wait()
        out_i[t] = in1[t, 0:HALF, :].astype(F32)
        put(out_i.at[t], w_in.at[:, pl.ds(t * MODEL, MODEL)], 4 + t)
        lines = pl.ds(t * QUARTER, QUARTER)
        out_o[lines, :] = in1[t, HALF : HALF + QUARTER, :].astype(F32)
        put(out_o.at[lines], w_out.at[lines], 8 + t)
    for pair in range(2):
        loads[2 * TILES + 2 * pair].wait()
        loads[2 * TILES + 2 * pair + 1].wait()
        for j, first in enumerate((0, 256, 448)):
            out_q[:, j * MODEL + pair * HALF : j * MODEL + (pair + 1) * HALF] = (
                jnp.concatenate(
                    [
                        in2[2 * pair + i].astype(F32)[:, first : first + LANES]
                        for i in range(2)
                    ],
                    axis=1,
                )
            )
    put(out_q, w_qkv, 12)
    for store in stores:
        store.wait()


def unpack_call(*arrays):
    shape = jax.ShapeDtypeStruct
    vmem = pl.BlockSpec(memory_space=pltpu.VMEM)
    hbm = pl.BlockSpec(memory_space=pltpu.HBM)
    vector = (shape((HALF,), F32), vmem)
    outs = [
        (shape((BLOCK, MODEL), BF16), hbm),
        (shape((BLOCK, MODEL), F32), hbm),
        (shape((HALF, 3 * MODEL), F32), hbm),
        vector,
        vector,
        (shape((HALF, MODEL), F32), hbm),
        vector,
        vector,
        vector,
        (shape((HALF, FF), F32), hbm),
        (shape((FF // 2,), F32), vmem),
        (shape((FF // 2, MODEL), F32), hbm),
        vector,
        vector,
        vector,
    ]
    return pl.pallas_call(
        unpack_kernel,
        out_shape=[o[0] for o in outs],
        in_specs=[vmem, vmem, hbm, hbm, hbm, vmem],
        out_specs=[o[1] for o in outs],
        scratch_shapes=[
            pltpu.VMEM((TILES, rows, width), BF16)
            for rows, width in zip(SET_ROWS, SET_WIDTH)
        ]
        + [
            pltpu.VMEM((HALF, 3 * MODEL), F32),
            pltpu.VMEM((HALF, MODEL), F32),
            pltpu.VMEM((TILES, HALF, MODEL), F32),
            pltpu.VMEM((FF // 2, MODEL), F32),
            pltpu.SemaphoreType.DMA((3 * TILES,)),
            pltpu.SemaphoreType.DMA((16,)),
        ],
        compiler_params=pltpu.CompilerParams(vmem_limit_bytes=60 * 2**20),
        name="unpack",
    )(*arrays)


def body(*args):
    planes = lax.axis_size("ctx") // GROUP
    result, d_tokens, *rest = unpack_call(*layer_call(planes, args))
    return (result[None], d_tokens[None], *rest)


def solution(mesh):
    token_spec = P("wsh", "ctx", None)
    matrix, vector = P("wsh", None), P("wsh")
    in_specs = (
        token_spec,
        P("wsh", "ctx"),
        matrix,
        vector,
        vector,
        matrix,
        vector,
        vector,
        vector,
        matrix,
        vector,
        matrix,
        vector,
        vector,
        vector,
        token_spec,
    )
    out_specs = (
        token_spec,
        token_spec,
        matrix,
        vector,
        vector,
        matrix,
        vector,
        vector,
        vector,
        matrix,
        vector,
        matrix,
        vector,
        vector,
        vector,
    )
    return jax.shard_map(body, mesh=mesh, in_specs=in_specs, out_specs=out_specs, check_vma=False)
```

time: 1590 us -> 200 us (0.13)
  waiting for transfers between devices: 608 us -> 0 us
  blocking collectives: 337 us -> 0 us
  other arithmetic: 326 us -> 0 us
  Pallas kernels: 0 us -> 199 us
  local copies, waits for them, and re-layouts: 183 us -> 0 us
  matrix products: 79.7 us -> 0 us
  starting transfers between devices: 28.9 us -> 0 us
    unnamed x7 -> x0, waiting for transfers between devices: 320 us -> none
    unnamed x1 -> x0, blocking collectives: 298 us -> none
    pallas_call x0 -> x2, Pallas kernels: none -> 199 us  [the longest x1 189 us: layer_call(): pl.pallas_call(functools.partial(layer_kernel, planes, list(buffers), lis...]
    convert_element_type x30 -> x0, other arithmetic: 182 us -> none  [the longest x1 153 us: body(): summed_flat = lax.all_gather(own_part.astype(jnp.bfloat16), 'ctx', axis=0...]
    all_gather x5 -> x0, waiting for transfers between devices: 170 us -> none  [the longest x1 112 us: body(): lax.all_gather(own_part.astype(jnp.bfloat16), 'ctx', axis=0, tiled=True)]
    another operation x2 -> x0, other arithmetic: 130 us -> none  [the longest x1 130 us: body(): spread_shard = spread_shard.reshape(ctx_count, piece_len)]
    ppermute x69 -> x0, waiting for transfers between devices: 118 us -> none  [passed_along(): lax.ppermute(value, axis, [(i, (i + by) % length) for i in range(length)])]
    dot_general x75 -> x0, matrix products: 79.7 us -> none  [the longest x9 14.7 us: back_visit(): jnp.einsum('hqk,qhd->khd', d_score, queries, preferred_element_type=jnp.f...]
  transfers between devices with their start and end apart: 75 -> 0, of which waited for: 28 -> 0; matrix products, arithmetic and copies ran while one was open for 8% -> 0% of each run, Pallas kernels for 0% -> 0%
where the time goes in v1:
time: 200 us
  Pallas kernels  199 us (100%)
    pallas_call x1, Pallas kernels, layer_call(): pl.pallas_call(functools.partial(layer_kernel, planes, list(buffers), lis...  189 us
    pallas_call x1, Pallas kernels, unpack_call(): pl.pallas_call(unpack_kernel, out_shape=[o[0] for o in outs], in_specs=[v...  9.86 us

profile of v1, /device:TPU:0, one launch (start us, length us, event | category | flops | bytes accessed | tf_op | source)
XLA Modules:
  0.0 199.9 jit_solution(2667023468855429491)
XLA Ops:
  0.7 189.3 %layer.1 = (bf16[128,768]{1,0:T(8,128)(2,1)}, f32[128,768]{1,0:T(8,128)}, bf16[1536,768]{1,0:T(8,128)(2,1)}, bf16[2048,768]{1,0:T(8,128)(2,1)}, bf16[1536,640]{1,0:T(8,128)(2,1)}, /*index=5*/f32[24,768]{1,0:T(8,128)}) custom-call(bf16[1,128,768]{2,1,0:T(8,128)(2,1)} %refs_0_.1, s32[1,128]{1,0:T(1,128)} %refs_1_.1, bf16[384,2304]{1,0:T(8,128)(2,1)} %refs_2_.1, ...), custom_call_target="tpu_custom_call" | custom-call | tf_op jit(solution)/shard_map/layer/pallas_call | solution.py:1017
  189.9 9.9 %unpack.1 = (bf16[128,768]{1,0:T(8,128)(2,1)}, f32[128,768]{1,0:T(8,128)}, f32[384,2304]{1,0:T(8,128)}, f32[384]{0:T(512)}, f32[384]{0:T(512)}, /*index=5*/f32[3...) custom-call(bf16[128,768]{1,0:T(8,128)(2,1)} %get-tuple-element.36.r, ...), custom_call_target="tpu_custom_call" | custom-call | tf_op jit(solution)/shard_map/unpack/pallas_call | solution.py:1127

commit v2 on v1

--- a/solution.py
+++ b/solution.py
@@ -126,13 +126,11 @@
         bias2=((2, 16, HALF), BF16),
         dout_far=((BLOCK, MODEL), BF16),
         ids=((3, GROUP, 8, BLOCK), F32),
-        acc=((BLOCK, 3 * MODEL), F32),
-        qsend=((GROUP, BLOCK, 256), BF16),
-        kvsend=((GROUP, BLOCK, 2 * LANES), BF16),
+        acc=((PLANE, 3 * 256), F32),
         qp=((PLANE, 256), BF16),
         kv=((3 * PLANE, 2 * LANES), BF16),
-        og=((PLANE, 256), F32),
-        lse=((PLANE, BLOCK), F32),
+        out_t=((GROUP_HEADS, HEAD_DIM, PLANE), F32),
+        peaks=((2 * GROUP_HEADS, 8, PLANE), F32),
         asend=((GROUP, BLOCK, 256), BF16),
         arecv=((GROUP, BLOCK, 256), BF16),
         tok_plane=((PLANE, MODEL), BF16),
@@ -173,10 +171,16 @@
             buffers[f"y_send{g}"] = ((rows, width), BF16)
             buffers[f"y_recv{g}"] = ((rows, width), BF16)
         buffers[f"z_send{g}"] = ((rows, width), BF16)
-        buffers[f"z_recv{g}"] = ((planes, chunk, width), BF16)
+        buffers[f"up_recv{g}"] = ((rows, width), BF16)
+        buffers[f"down_recv{g}"] = ((rows, width), BF16)
         buffers[f"final{g}"] = ((chunk, width), BF16)
     semaphores = dict(
         local=(4 + 3,),
+        qx=(3,),
+        qz=(3,),
+        qc=(2, 3),
+        late_x=(3,),
+        late_c=(3,),
         wx=(4, 2),
         wy=(4, 2),
         wz=(4, 2),
@@ -189,7 +193,8 @@
         core=(4,),
         xs=(planes,),
         ys=(2, planes),
-        zs=(3, planes),
+        up=(3, planes),
+        down=(3, planes),
         gu=(3, planes),
         gd=(3, planes),
         gy=(3, planes),
@@ -223,6 +228,7 @@
         return pl.ds(pl.multiple_of(first + i * BLOCK, BLOCK), BLOCK)
 
     b.ids[1, at.r] = jnp.broadcast_to(b.doc_ids[...].astype(F32), (8, BLOCK))
+    b.tok_plane[block_rows(0, at.r), :] = b.tokens[0]
 
     @pl.when(jnp.logical_not(at.has_down))
     def _():
@@ -250,7 +256,7 @@
 
     shards = (b.w_qkv, b.w_out, b.w_in, b.w_back)
     wholes = (b.wq, b.wo, b.wi, b.wb)
-    direct = (True, True, False, False)
+    direct = (True, True, True, False)
     own_q = at.y * 2 + at.parity
     diag_q = (1 - at.y) * 2 + (1 - at.parity)
     beside_q = (1 - at.y) * 2 + at.parity
@@ -325,12 +331,50 @@
     bias_copy = remote(b.bias_own, b.bias2.at[at.x], s.ex, 0, at.across)
     tok_copy = remote(b.tokens.at[0], b.tok2.at[far_tokens], s.ex, 1, at.across)
     dout_copy = remote(b.d_out.at[0], b.dout_far, s.ex, 2, at.across)
-    for i in range(2):
-        start(across_copy(0, i))
-    start(bias_copy)
-    for d in (1, 2, 3):
-        mine = b.ids.at[1, at.r]
-        start(remote(mine, mine, s.a2a, (0, d), at.in_plane(at.peer(d))))
+    def q_piece(ref, first_row, size, j, side):
+        return ref.at[
+            pl.ds(pl.multiple_of(first_row, 16), size),
+            pl.ds(pl.multiple_of(j * MODEL + side * HALF, 128), HALF),
+        ]
+
+    def q_rows(core, parity):
+        return (core * 2 + parity) * QUARTER
+
+    far_base = (1 - at.x) * HALF
+    near_base = at.x * HALF
+
+    def q_across(j):
+        line = q_rows(at.k, at.parity)
+        return remote(
+            q_piece(b.w_qkv, line, QUARTER, j, at.y),
+            q_piece(b.wq, near_base + line, QUARTER, j, at.y),
+            s.qx,
+            j,
+            at.across,
+        )
+
+    def q_move(core, parity, j, sems, index, device):
+        piece = q_piece(b.wq, far_base + q_rows(core, parity), QUARTER, j, at.y)
+        return remote(piece, piece, sems, index, device)
+
+    def late_across(j):
+        line = at.k * 2 * QUARTER
+        return remote(
+            q_piece(b.w_qkv, line, 2 * QUARTER, j, 1 - at.y),
+            q_piece(b.wq, near_base + line, 2 * QUARTER, j, 1 - at.y),
+            s.late_x,
+            j,
+            at.across,
+        )
+
+    def late_move(core, j, sems, device):
+        piece = q_piece(b.wq, far_base + core * 2 * QUARTER, 2 * QUARTER, j, 1 - at.y)
+        return remote(piece, piece, sems, j, device)
+
+    def tok_block(i, sem, device):
+        piece = b.tok_plane.at[block_rows(0, i)]
+        return remote(piece, piece, s.tp, sem, device)
+
     own_copies = []
     for w in range(4):
         size = shards[w].shape[0]
@@ -341,70 +385,72 @@
                 s.local[0].at[w],
             )
         )
+    for j in range(3):
+        start(q_across(j))
+    start(bias_copy)
+    start(tok_block(at.r, 0, at.beside))
+    start(tok_block(at.r, 1, at.sister))
     own_copies[0].start()
+    for d in (1, 2, 3):
+        mine = b.ids.at[1, at.r]
+        start(remote(mine, mine, s.a2a, (0, d), at.in_plane(at.peer(d))))
 
     near_rows = pl.multiple_of(at.x * HALF, HALF)
     far_rows = pl.multiple_of((1 - at.x) * HALF, HALF)
     b.tok2[near_tokens, :] = b.tokens[0]
-    b.tok_plane[block_rows(0, at.r), :] = b.tokens[0]
-    own_copies[0].wait()
-    near = b.tokens[0, :, pl.ds(near_rows, HALF)]
     for j in range(3):
-        cols = slice(j * MODEL, (j + 1) * MODEL)
-        b.acc[:, cols] = jnp.dot(
-            near, b.wq[pl.ds(near_rows, HALF), cols], preferred_element_type=F32
-        )
+        q_move(at.k, at.parity, j, s.qx, j, at.across).wait_recv()
+        start(q_move(at.k, at.parity, j, s.qz, j, at.pair))
+        start(q_move(at.k, at.parity, j, s.qc, (0, j), at.sister))
+    start(across_copy(2, 0))
+    for i in range(2):
+        start(across_copy(1, i))
+    start(across_copy(3, 0))
+    start(across_copy(2, 1))
+    start(tok_copy)
     for w in (1, 2, 3):
         own_copies[w].start()
-    relay_own(0)
-    relay_rest(0)
-    for i in range(2):
-        start(across_copy(1, i))
-    start(across_copy(2, 0))
+    tok_block(at.peer(2), 0, at.beside).wait_recv()
+    start(tok_block(at.peer(2), 2, at.sister))
+    for j in range(3):
+        q_move(at.k, 1 - at.parity, j, s.qz, j, at.pair).wait_recv()
+        start(q_move(at.k, 1 - at.parity, j, s.qc, (1, j), at.sister))
+    tok_block(at.peer(1), 1, at.sister).wait_recv()
+    tok_block(at.peer(3), 2, at.sister).wait_recv()
+    own_copies[0].wait()
+    window = [
+        pl.ds(pl.multiple_of(j * MODEL + at.y * HALF + at.k * 128, 128), 256) for j in range(3)
+    ]
+    for j in range(3):
+        b.acc[:, j * 256 : (j + 1) * 256] = jnp.dot(
+            b.tok_plane[:, pl.ds(near_rows, HALF)],
+            b.wq[pl.ds(near_rows, HALF), window[j]],
+            preferred_element_type=F32,
+        )
     remote(b.bias_own, b.bias2.at[1 - at.x], s.ex, 0, at.across).wait_recv()
     halves = (b.bias2[0].astype(F32), b.bias2[1].astype(F32))
     bias = jnp.concatenate(halves, axis=1)
-    sister_arrivals(0)
-    apart = b.tokens[0, :, pl.ds(far_rows, HALF)]
+
+    def group_bias(row):
+        line = bias[row : row + 1, 0:LANES]
+        for g in range(1, GROUP):
+            line = jnp.where(at.r == g, bias[row : row + 1, g * LANES : (g + 1) * LANES], line)
+        return line
+
     for j in range(3):
-        cols = slice(j * MODEL, (j + 1) * MODEL)
-        part = b.acc[:, cols] + jnp.dot(
-            apart, b.wq[pl.ds(far_rows, HALF), cols], preferred_element_type=F32
-        )
-        if j == 0:
-            part = part + bias[0:1]
-        if j == 2:
-            part = part + bias[1:2]
-        b.acc[:, cols] = part
-
-    zero_lanes = jnp.zeros((BLOCK, HEAD_DIM), F32)
-    for g in range(GROUP):
-        cols = [
-            b.acc[:, j * MODEL + g * LANES : j * MODEL + (g + 1) * LANES] for j in range(3)
-        ]
-        b.qsend[g] = jnp.concatenate([cols[0], zero_lanes], axis=1).astype(BF16)
-        b.kvsend[g] = jnp.concatenate([cols[1], cols[2]], axis=1).astype(BF16)
-
-    for d in (1, 2, 3):
-        g = at.peer(d)
-        start(
-            remote(
-                b.kvsend.at[g],
-                b.kv.at[block_rows(PLANE, at.r)],
-                s.a2a,
-                (1, d),
-                at.in_plane(g),
-            )
-        )
-    for d in (1, 2, 3):
-        g = at.peer(d)
-        start(
-            remote(
-                b.qsend.at[g], b.qp.at[block_rows(0, at.r)], s.a2a, (2, d), at.in_plane(g)
-            )
-        )
-    b.kv[block_rows(PLANE, at.r), :] = b.kvsend[at.r]
-    b.qp[block_rows(0, at.r), :] = b.qsend[at.r]
+        q_move(1 - at.k, at.parity, j, s.qc, (0, j), at.sister).wait_recv()
+        q_move(1 - at.k, 1 - at.parity, j, s.qc, (1, j), at.sister).wait_recv()
+    made = []
+    for j in range(3):
+        part = b.acc[:, j * 256 : (j + 1) * 256] + jnp.dot(
+            b.tok_plane[:, pl.ds(far_rows, HALF)],
+            b.wq[pl.ds(far_rows, HALF), window[j]],
+            preferred_element_type=F32,
+        )
+        made.append(jnp.where(at.k == 0, part[:, 0:LANES], part[:, HEAD_DIM:256]))
+    b.kv[pl.ds(PLANE, PLANE), :] = jnp.concatenate(
+        [made[1], made[2] + group_bias(1)], axis=1
+    ).astype(BF16)
 
     def both_ways(up, down, act):
         @pl.when(at.has_up)
@@ -418,95 +464,99 @@
     def go(copy):
         copy.start()
 
-    def block_of(d):
-        return at.r if d == 0 else at.peer(d)
-
-    def up_kv(d):
-        i = block_of(d)
-        return remote(
-            b.kv.at[block_rows(PLANE, i)], b.kv.at[block_rows(0, i)], s.halo_f, (0, d), at.up
-        )
-
-    def down_kv(d):
-        i = block_of(d)
-        return remote(
-            b.kv.at[block_rows(PLANE, i)],
-            b.kv.at[block_rows(2 * PLANE, i)],
-            s.halo_f,
-            (1, d),
-            at.down,
-        )
-
-    up_ids = remote(b.ids.at[1], b.ids.at[0], s.halo_f, (0, 4), at.up)
-    down_ids = remote(b.ids.at[1], b.ids.at[2], s.halo_f, (1, 4), at.down)
+    middle = b.kv.at[pl.ds(PLANE, PLANE)]
+    up_kv = remote(middle, b.kv.at[pl.ds(0, PLANE)], s.halo_f, (0, 0), at.up)
+    down_kv = remote(middle, b.kv.at[pl.ds(2 * PLANE, PLANE)], s.halo_f, (1, 0), at.down)
+    up_ids = remote(b.ids.at[1], b.ids.at[0], s.halo_f, (0, 1), at.up)
+    down_ids = remote(b.ids.at[1], b.ids.at[2], s.halo_f, (1, 1), at.down)
 
     def from_peer(piece, kind, d):
         remote(piece, piece, s.a2a, (kind, d), at.in_plane(at.peer(d))).wait_recv()
 
-    both_ways(up_kv(0), down_kv(0), go)
+    both_ways(up_kv, down_kv, go)
+    b.qp[...] = jnp.concatenate(
+        [made[0] + group_bias(0), jnp.zeros((PLANE, HEAD_DIM), F32)], axis=1
+    ).astype(BF16)
     for d in (1, 2, 3):
         from_peer(b.ids.at[1, at.peer(d)], 0, d)
     both_ways(up_ids, down_ids, go)
+
+    q_ids = jnp.concatenate([b.ids[1, j][0:1, :] for j in range(GROUP)], axis=1)
+    peaks = b.peaks
+
+    def key_ids(i):
+        for j in range(GROUP):
+            b.k_ids[(i * GROUP + j) * BLOCK : (i * GROUP + j + 1) * BLOCK, :] = column_of(
+                b.ids[i, j][0:1, :]
+            )
+
+    def attend(i):
+        key_ids(i)
+        span = pl.ds(i * PLANE, PLANE)
+        same = b.k_ids[span, 0:1] == q_ids
+        for h in range(GROUP_HEADS):
+            q = b.qp[...] * SCALE
+            q = jnp.where(lane_head((PLANE, 256), 0) == h, q, jnp.zeros_like(q))
+            score = lax.dot_general(b.kv[span, 0:256], q, NT, preferred_element_type=F32)
+            score = jnp.where(same, score, NEGATIVE)
+            peak = jnp.max(score, axis=0, keepdims=True)
+            if i != 1:
+                old = peaks[h][0:1, :]
+                peak = jnp.maximum(peak, old)
+                factor = jnp.exp(old - peak)
+            weight = jnp.exp(score - peak)
+            summed = jnp.sum(weight, axis=0, keepdims=True)
+            first_lane, line = ((128, HEAD_DIM), (256, 0), (256, HEAD_DIM))[h]
+            out = lax.dot_general(
+                b.kv[span, first_lane : first_lane + 128],
+                weight.astype(BF16),
+                TN,
+                preferred_element_type=F32,
+            )[line : line + HEAD_DIM, :]
+            if i != 1:
+                out = out + b.out_t[h] * factor
+                summed = summed + peaks[GROUP_HEADS + h][0:1, :] * factor
+            b.out_t[h] = out
+            peaks[h] = jnp.broadcast_to(peak, (8, PLANE))
+            peaks[GROUP_HEADS + h] = jnp.broadcast_to(summed, (8, PLANE))
+
+    relay_own(2)
+    attend(1)
     relay_own(1)
-    for d in (1, 2, 3):
-        from_peer(b.kv.at[block_rows(PLANE, at.peer(d))], 1, d)
-        both_ways(up_kv(d), down_kv(d), go)
-    relay_rest(1)
-    relay_own(2)
-    start(across_copy(3, 0))
-    start(tok_copy)
-    for d in (1, 2, 3):
-        from_peer(b.qp.at[block_rows(0, at.peer(d))], 2, d)
-    relay_rest(2)
 
     @pl.when(at.has_down)
     def _():
-        for d in range(4):
-            piece = b.kv.at[block_rows(0, block_of(d))]
-            remote(piece, piece, s.halo_f, (0, d), at.down).wait_recv()
-        remote(b.ids.at[0], b.ids.at[0], s.halo_f, (0, 4), at.down).wait_recv()
+        came = b.kv.at[pl.ds(0, PLANE)]
+        remote(came, came, s.halo_f, (0, 0), at.down).wait_recv()
+        remote(b.ids.at[0], b.ids.at[0], s.halo_f, (0, 1), at.down).wait_recv()
+
+    attend(0)
 
     @pl.when(at.has_up)
     def _():
-        for d in range(4):
-            piece = b.kv.at[block_rows(2 * PLANE, block_of(d))]
-            remote(piece, piece, s.halo_f, (1, d), at.up).wait_recv()
-        remote(b.ids.at[2], b.ids.at[2], s.halo_f, (1, 4), at.up).wait_recv()
-
-    def attend(t, carry):
-        q_rows = block_rows(0, t)
-        q_ids = column_of(b.ids[1, t][0:1, :])[:, 0:1]
-        k_ids = jnp.concatenate(
-            [b.ids[i, j][0:1, :] for i in range(3) for j in range(GROUP)], axis=1
-        )
-        same = q_ids == k_ids
-        total = jnp.zeros((BLOCK, 256), F32)
-        logs = jnp.zeros((BLOCK, BLOCK), F32)
-        for h in range(GROUP_HEADS):
-            q = b.qp[q_rows, :] * SCALE
-            q = jnp.where(lane_head((BLOCK, 256), 0) == h, q, jnp.zeros_like(q))
-            score = lax.dot_general(q, b.kv[:, 0:256], NT, preferred_element_type=F32)
-            score = jnp.where(same, score, NEGATIVE)
-            peak = jnp.max(score, axis=1, keepdims=True)
-            weight = jnp.exp(score - peak)
-            summed = jnp.sum(weight, axis=1, keepdims=True)
-            out = jnp.dot(weight.astype(BF16), b.kv[:, 128:384], preferred_element_type=F32)
-            out = out / summed
-            total = jnp.where(lane_head((BLOCK, 256), 1) == h, out, total)
-            lane = lax.broadcasted_iota(jnp.int32, (BLOCK, BLOCK), 1)
-            logs = jnp.where(lane == h, peak + jnp.log(summed), logs)
-        b.og[q_rows, :] = total
-        b.lse[q_rows, :] = logs
-        b.asend[t] = total.astype(BF16)
-        return carry
-
-    lax.fori_loop(0, GROUP, attend, 0)
+        came = b.kv.at[pl.ds(2 * PLANE, PLANE)]
+        remote(came, came, s.halo_f, (1, 0), at.up).wait_recv()
+        remote(b.ids.at[2], b.ids.at[2], s.halo_f, (1, 1), at.up).wait_recv()
+
+    attend(2)
+    outs = [jnp.zeros((HEAD_DIM, PLANE), F32)]
+    for h in range(GROUP_HEADS):
+        summed = peaks[GROUP_HEADS + h][0:1, :]
+        out = b.out_t[h] / summed
+        b.out_t[h] = out
+        b.stats[h] = peaks[h] + jnp.log(peaks[GROUP_HEADS + h])
+        outs.append(out)
+    attended = jnp.concatenate(outs, axis=0).T.astype(BF16)
+    for i in range(GROUP):
+        b.asend[i] = attended[i * BLOCK : (i + 1) * BLOCK, :]
 
     for d in (1, 2, 3):
         i = at.peer(d)
         start(remote(b.asend.at[i], b.arecv.at[at.r], s.a2a, (3, d), at.in_plane(i)))
     b.arecv[at.r] = b.asend[at.r]
     relay_own(3)
+    relay_rest(1)
+    relay_rest(2)
     for d in (1, 2, 3):
         from_peer(b.arecv.at[at.peer(d)], 3, d)
     b.att2[near_tokens, :] = jnp.concatenate(
@@ -515,10 +565,9 @@
     att_copy = remote(b.att2.at[near_tokens], b.att2.at[far_tokens], s.ex, 3, at.across)
     start(att_copy)
     start(dout_copy)
+    sister_arrivals(1)
     relay_rest(3)
-    relay_diagonal(2)
     own_copies[1].wait()
-    sister_arrivals(1)
     tok_copy.wait_recv()
     att_copy.wait_recv()
 
@@ -538,12 +587,6 @@
     def column_sum(value):
         return jnp.sum(value, axis=0, keepdims=True)
 
-    def tok_block(i, sem, device):
-        piece = b.tok_plane.at[block_rows(0, i)]
-        return remote(piece, piece, s.tp, sem, device)
-
-    start(tok_block(at.r, 0, at.beside))
-    start(tok_block(at.r, 1, at.sister))
     first = (
         b.tok2[...].astype(F32)
         + jnp.dot(b.att2[...], b.wo[...], preferred_element_type=F32)
@@ -629,17 +672,31 @@
             at.beside,
         )
 
-    def z_copy(group, j):
+    def up_copy(group, j):
+        lines = chunk_rows(group, j)
         return remote(
-            of("z_send", group).at[chunk_rows(group, j)],
-            of("z_recv", group).at[at.p],
-            s.zs,
+            of("z_send", group).at[lines],
+            of("up_recv", group).at[lines],
+            s.up,
             (group, j),
-            at.plane(j),
-            (group, at.p),
-        )
-
-    def each_owner(group, act, first=1):
+            at.up,
+        )
+
+    def down_copy(group, j):
+        lines = chunk_rows(group, j)
+        return remote(
+            of("z_send", group).at[lines],
+            of("down_recv", group).at[lines],
+            s.down,
+            (group, j),
+            at.down,
+        )
+
+    middle_step = planes // 2 + 1
+    early, late = (1, middle_step), (middle_step, planes + 1)
+    whole_way = (1, planes + 1)
+
+    def each_owner(group, act, span):
         def one(d, carry):
             j = (at.p + d) % planes
 
@@ -649,19 +706,25 @@
 
             return carry
 
-        lax.fori_loop(first, first + planes, one, 0)
-
-    def produce(group):
+        lax.fori_loop(*span, one, 0)
+
+    def make(group):
         base = OWN_ROWS[group]
         for i, t in enumerate((at.peer(3), at.peer(1))):
             of("core_send", group)[i, 0:HALF, :] = tile(group, t).astype(BF16)
             if group == 1:
                 of("core_send", group)[i, HALF : HALF + QUARTER, :] = out_quarter(t).astype(BF16)
             start(core_copy(group, i))
-        passing = tile(group, at.peer(2))
         b.slope[base : base + HALF, :] = tile(group, at.r)
         if group == 1:
             b.slope[base + HALF : base + HALF + QUARTER, :] = out_quarter(at.r)
+
+    def go_over_y(group, span):
+        each_owner(group, lambda j: y_copy(group, j).start(), span)
+
+    def exchange(group):
+        base = OWN_ROWS[group]
+        passing = tile(group, at.peer(2))
         core_copy(group, 0).wait_recv()
         come = of("core_recv", group)
         of("y_send", group)[0:HALF, :] = (passing + come[0, 0:HALF, :].astype(F32)).astype(BF16)
@@ -671,12 +734,12 @@
             of("y_send", group)[lines, :] = (
                 out_quarter(at.peer(2)) + come[0, lines, :].astype(F32)
             ).astype(BF16)
-        each_owner(group, lambda j: y_copy(group, j).start())
+        go_over_y(group, early)
         core_copy(group, 1).wait_recv()
         used = SET_ROWS[0] if group == 0 else HALF + QUARTER
         b.slope[base : base + used, :] += come[1, 0:used, :].astype(F32)
 
-    def scatter(group):
+    def scatter(group, span):
         def act(j):
             mine = own_chunk(group, j)
             if group == 2:
@@ -688,16 +751,60 @@
             total = mine[...] + came.astype(F32)
             mine[...] = total
 
-            @pl.when(j != at.p)
+            @pl.when(jnp.logical_and(at.p == 0, j > 0))
             def _():
                 of("z_send", group)[chunk_rows(group, j), :] = total.astype(BF16)
-                z_copy(group, j).start()
-
-        each_owner(group, act)
+                up_copy(group, j).start()
+
+            @pl.when(jnp.logical_and(at.p == planes - 1, j < planes - 1))
+            def _():
+                of("z_send", group)[chunk_rows(group, j), :] = total.astype(BF16)
+                down_copy(group, j).start()
+
+        each_owner(group, act, span)
+
+    def add_arrived(group, j, name, sems, device):
+        lines = chunk_rows(group, j)
+        came = of(name, group).at[lines]
+        remote(came, came, sems, (group, j), device).wait_recv()
+        return came[...].astype(F32)
+
+    def relay_sums(group, h):
+        @pl.when(at.p == h)
+        def _():
+            def one(i, carry):
+                j = owners[group] - 1 - i
+                total = own_chunk(group, j)[...] + add_arrived(
+                    group, j, "up_recv", s.up, at.down
+                )
+                of("z_send", group)[chunk_rows(group, j), :] = total.astype(BF16)
+                up_copy(group, j).start()
+                return carry
+
+            lax.fori_loop(0, owners[group] - 1 - at.p, one, 0)
+
+        @pl.when(at.p == planes - 1 - h)
+        def _():
+            def one(j, carry):
+                total = own_chunk(group, j)[...] + add_arrived(
+                    group, j, "down_recv", s.down, at.up
+                )
+                of("z_send", group)[chunk_rows(group, j), :] = total.astype(BF16)
+                down_copy(group, j).start()
+                return carry
+
+            lax.fori_loop(0, jnp.minimum(at.p, owners[group]), one, 0)
 
     def x_copy(j):
         lines = chunk_rows(2, j)
         return remote(b.x_send.at[lines], b.x_recv.at[lines], s.xs, j, at.across)
+
+    def more_sums(group):
+        def one(h, carry):
+            relay_sums(group, h)
+            return carry
+
+        lax.fori_loop(3, planes - 1, one, 0)
 
     def place(group, t, j):
         first_row = t * SET_ROWS[group] + j * chunks[group]
@@ -727,42 +834,57 @@
     def settle(group):
         @pl.when(at.p < owners[group])
         def _():
-            came = of("z_recv", group)
-
-            def add(d, total):
-                q = (at.p + d) % planes
-                remote(came.at[q], came.at[q], s.zs, (group, q), at.plane(q)).wait_recv()
-                return total + came[q].astype(F32)
-
-            total = lax.fori_loop(1, planes, add, own_chunk(group, at.p)[...])
+            mine = own_chunk(group, at.p)
+
+            @pl.when(at.has_down)
+            def _():
+                mine[...] += add_arrived(group, at.p, "up_recv", s.up, at.down)
+
+            @pl.when(at.has_up)
+            def _():
+                mine[...] += add_arrived(group, at.p, "down_recv", s.down, at.up)
+
+            total = mine[...]
             of("final", group)[...] = total.astype(BF16)
             spread(group, at.p, of("final", group))
             settle_copy(group).start()
 
-    def come_in(group):
-        def one(d, carry):
-            @pl.when(jnp.logical_and(at.p - d >= 0, at.p - d < owners[group]))
-            def _():
-                gather_copy(group, at.r, at.p - d, s.gu, at.down).wait_recv()
-                spread(group, at.p - d)
-
-            @pl.when(at.p + d < owners[group])
-            def _():
-                gather_copy(group, at.r, at.p + d, s.gd, at.up).wait_recv()
-                spread(group, at.p + d)
-
-            return carry
-
-        lax.fori_loop(1, planes, one, 0)
-
-    def hand_over(group):
-        def act(j):
+    def around(group, d, act):
+        @pl.when(jnp.logical_and(at.p - d >= 0, at.p - d < owners[group]))
+        def _():
+            act(at.p - d, s.gu, at.down)
+
+        @pl.when(jnp.logical_and(d > 0, at.p + d < owners[group]))
+        def _():
+            act(at.p + d, s.gd, at.up)
+
+    def come_in(group, d):
+        def act(j, sems, device):
+            gather_copy(group, at.r, j, sems, device).wait_recv()
+            spread(group, j)
+
+        around(group, d, act)
+
+    def hand_over(group, d):
+        def act(j, sems, device):
             gather_copy(group, at.peer(2), j, s.gy, at.beside).wait_recv()
             gather_copy(group, at.peer(2), j, s.gf, at.sister).start()
 
-        each_owner(group, act, 0)
-
+        around(group, d, act)
+
+    def more_gathers():
+        def one(d, carry):
+            for group in range(3):
+                come_in(group, d)
+                hand_over(group, d)
+            return carry
+
+        lax.fori_loop(4, planes, one, 0)
+
+    make(0)
     for c in range(4):
+        if c == 2:
+            exchange(0)
         cols = slice(c * MODEL, (c + 1) * MODEL)
         d_inner = (
             lax.dot_general(b.d_second[...], b.wb[cols, :], NT, preferred_element_type=F32)
@@ -784,7 +906,7 @@
     d_attn = lax.dot_general(d_first_low[:BLOCK], b.wo[...], NT, preferred_element_type=F32)
     for g in range(GROUP):
         b.dsend[g] = jnp.concatenate(
-            [zero_lanes, d_attn[:, g * LANES : (g + 1) * LANES]], axis=1
+            [jnp.zeros((BLOCK, HEAD_DIM), F32), d_attn[:, g * LANES : (g + 1) * LANES]], axis=1
         ).astype(BF16)
     for d in (1, 2, 3):
         g = at.peer(d)
@@ -793,28 +915,25 @@
                 b.dsend.at[g], b.do.at[block_rows(0, at.r)], s.a2a, (4, d), at.in_plane(g)
             )
         )
+    go_over_y(0, late)
     b.do[block_rows(0, at.r), :] = b.dsend[at.r]
 
-    tok_block(at.peer(2), 0, at.beside).wait_recv()
-    start(tok_block(at.peer(2), 2, at.sister))
-    produce(0)
+    for j in range(3):
+        start(late_across(j))
+    b.out_tile[...] = lax.dot_general(
+        b.att2[:, pl.ds(near_rows, HALF)], b.d_first[...], TN, preferred_element_type=F32
+    )
+    make(1)
 
     b.grads[...] = jnp.zeros_like(b.grads)
     b.dq[...] = jnp.zeros_like(b.dq)
-    for i in range(3):
-        for j in range(GROUP):
-            b.k_ids[(i * GROUP + j) * BLOCK : (i * GROUP + j + 1) * BLOCK, :] = column_of(
-                b.ids[i, j][0:1, :]
-            )
-    q_ids = jnp.concatenate([b.ids[1, j][0:1, :] for j in range(GROUP)], axis=1)
-    lse_rows = b.lse[...].T
     for d in (1, 2, 3):
         from_peer(b.do.at[block_rows(0, at.peer(d))], 4, d)
-    prod = (b.do[...].astype(F32) * b.og[...]).T
+    do_t = b.do[...].astype(F32).T
     for h in range(GROUP_HEADS):
-        b.stats[h] = jnp.broadcast_to(lse_rows[h : h + 1, :], (8, PLANE))
+        lines = slice(HEAD_DIM * (h + 1), HEAD_DIM * (h + 2))
         b.stats[GROUP_HEADS + h] = jnp.broadcast_to(
-            column_sum(prod[HEAD_DIM * (h + 1) : HEAD_DIM * (h + 2), :]), (8, PLANE)
+            column_sum(do_t[lines, :] * b.out_t[h]), (8, PLANE)
         )
 
     def visit(h, i):
@@ -847,6 +966,7 @@
 
     down_grads = remote(b.halo_send.at[0], b.halo.at[1], s.halo_b, 0, at.down)
     up_grads = remote(b.halo_send.at[1], b.halo.at[0], s.halo_b, 1, at.up)
+    scatter(0, early)
     visit_plane(0)
     b.halo_send[0] = b.grads[pl.ds(0, PLANE), :].astype(BF16)
 
@@ -854,6 +974,7 @@
     def _():
         down_grads.start()
 
+    exchange(1)
     visit_plane(2)
     b.halo_send[1] = b.grads[pl.ds(2 * PLANE, PLANE), :].astype(BF16)
 
@@ -861,12 +982,11 @@
     def _():
         up_grads.start()
 
+    scatter(0, late)
+    go_over_y(1, late)
     visit_plane(1)
     b.d_group[:, 0:256] = b.dq[...].astype(BF16)
-    b.out_tile[...] = lax.dot_general(
-        b.att2[:, pl.ds(near_rows, HALF)], b.d_first[...], TN, preferred_element_type=F32
-    )
-    produce(1)
+    relay_sums(0, 1)
 
     @pl.when(at.has_up)
     def _():
@@ -880,15 +1000,13 @@
 
     b.d_group[:, 256:640] = b.grads[pl.ds(PLANE, PLANE), :].astype(BF16)
 
-    tok_block(at.peer(1), 1, at.sister).wait_recv()
-    tok_block(at.peer(3), 2, at.sister).wait_recv()
+    b.line_send[...] = jnp.broadcast_to(column_sum(b.d_group[...].astype(F32)), (8, 640))
+    line_copy = remote(b.line_send, b.line_recv, s.ex, 4, at.across)
+    start(line_copy)
     b.x_send[...] = lax.dot_general(
         b.tok_plane[:, pl.ds(far_rows, HALF)], b.d_group[...], TN, preferred_element_type=F32
     ).astype(BF16)
-    each_owner(2, lambda j: x_copy(j).start())
-    b.line_send[...] = jnp.broadcast_to(column_sum(b.d_group[...].astype(F32)), (8, 640))
-    line_copy = remote(b.line_send, b.line_recv, s.ex, 4, at.across)
-    start(line_copy)
+    each_owner(2, lambda j: x_copy(j).start(), whole_way)
     for d in (1, 2, 3):
         i = at.peer(d)
         start(
@@ -904,9 +1022,6 @@
     b.q_sum[...] = lax.dot_general(
         b.tok_plane[:, pl.ds(near_rows, HALF)], b.d_group[...], TN, preferred_element_type=F32
     )
-    scatter(0)
-    scatter(2)
-
     partners = [at.sister, at.beside]
     span = 1
     while span < planes:
@@ -920,21 +1035,42 @@
         small_copy(i).wait()
         b.small[...] += b.small_recv[i]
 
+    relay_sums(0, 2)
+    scatter(1, early)
+    more_sums(0)
+    settle(0)
     line_copy.wait_recv()
     line = b.line_send[...] + b.line_recv[...]
     mine = lax.broadcasted_iota(jnp.int32, (8, 640), 0) == at.r
     b.small[16:24, 0:640] = jnp.where(mine, line, 0.0)
     small_copy(0).start()
-    settle(0)
+    scatter(1, late)
+    relay_sums(1, 1)
     small_finish(0)
     small_copy(1).start()
-    scatter(1)
+    come_in(0, 1)
+    scatter(2, early)
+    relay_sums(1, 2)
+    hand_over(0, 0)
+    scatter(2, late)
+    relay_sums(2, 1)
+    come_in(0, 2)
+    more_sums(1)
+    settle(1)
+    relay_sums(2, 2)
+    more_sums(2)
     small_finish(1)
     small_copy(2).start()
+    for j in range(3):
+        late_move(at.k, j, s.late_x, at.across).wait_recv()
+        start(late_move(at.k, j, s.late_c, at.sister))
+    hand_over(0, 1)
+    come_in(0, 3)
     settle(2)
-    come_in(0)
+    come_in(1, 1)
     small_finish(2)
     small_copy(3).start()
+    hand_over(0, 2)
 
     for d in (1, 2, 3):
         from_peer(b.d_recv.at[at.peer(d)], 5, d)
@@ -946,20 +1082,30 @@
             ],
             axis=1,
         ).astype(BF16)
+    for j in range(3):
+        late_move(1 - at.k, j, s.late_c, at.sister).wait_recv()
     b.d_tokens[...] += lax.dot_general(
         b.d_packed[...], b.wq[...], NT, preferred_element_type=F32
     )
-
-    hand_over(0)
+    come_in(1, 2)
+    come_in(2, 1)
+    hand_over(0, 3)
+    hand_over(1, 0)
+    come_in(1, 3)
+    come_in(2, 2)
+    hand_over(2, 0)
+    hand_over(1, 1)
+    come_in(2, 3)
     small_finish(3)
+    hand_over(2, 1)
+    hand_over(1, 2)
+    hand_over(2, 2)
+    hand_over(1, 3)
+    hand_over(2, 3)
+    more_gathers()
     for i in range(4, len(partners)):
         small_copy(i).start()
         small_finish(i)
-    settle(1)
-    come_in(2)
-    hand_over(2)
-    come_in(1)
-    hand_over(1)
 
     for group in range(3):
 
@@ -982,9 +1128,13 @@
             def _():
                 gather_copy(group, at.r, j, s.gd, at.down).wait_send()
 
-            @pl.when(j != at.p)
+            @pl.when(at.p < j)
             def _():
-                z_copy(group, j).wait_send()
+                up_copy(group, j).wait_send()
+
+            @pl.when(at.p > j)
+            def _():
+                down_copy(group, j).wait_send()
 
             return carry
 
@@ -1000,8 +1150,7 @@
     def finish(copy):
         copy.wait_send()
 
-    for d in range(4):
-        both_ways(up_kv(d), down_kv(d), finish)
+    both_ways(up_kv, down_kv, finish)
     both_ways(up_ids, down_ids, finish)
     both_ways(up_grads, down_grads, finish)
 

time: 200 us -> 168 us (0.84)
  Pallas kernels: 199 us -> 167 us
    pallas_call x1, Pallas kernels: 189 us -> 157 us  [layer_call(): pl.pallas_call(functools.partial(layer_kernel, planes, list(buffers), lis...]
where the time goes in v2:
time: 168 us; the launch traced here: 167 us
  Pallas kernels  167 us (99%)
    pallas_call x1, Pallas kernels, layer_call(): pl.pallas_call(functools.partial(layer_kernel, planes, list(buffers), lis...  157 us
    pallas_call x1, Pallas kernels, unpack_call(): pl.pallas_call(unpack_kernel, out_shape=[o[0] for o in outs], in_specs=[v...  9.86 us

profile of v2, /device:TPU:0, one launch (start us, length us, event | category | flops | bytes accessed | tf_op | source)
XLA Modules:
  0.0 167.4 jit_solution(12121800949141497767)
XLA Ops:
  0.7 156.7 %layer.1 = (bf16[128,768]{1,0:T(8,128)(2,1)}, f32[128,768]{1,0:T(8,128)}, bf16[1536,768]{1,0:T(8,128)(2,1)}, bf16[2048,768]{1,0:T(8,128)(2,1)}, bf16[1536,640]{1,0:T(8,128)(2,1)}, /*index=5*/f32[24,768]{1,0:T(8,128)}) custom-call(bf16[1,128,768]{2,1,0:T(8,128)(2,1)} %refs_0_.1, s32[1,128]{1,0:T(1,128)} %refs_1_.1, bf16[384,2304]{1,0:T(8,128)(2,1)} %refs_2_.1, ...), custom_call_target="tpu_custom_call" | custom-call | tf_op jit(solution)/shard_map/layer/pallas_call | solution.py:1166
  157.4 9.9 %unpack.1 = (bf16[128,768]{1,0:T(8,128)(2,1)}, f32[128,768]{1,0:T(8,128)}, f32[384,2304]{1,0:T(8,128)}, f32[384]{0:T(512)}, f32[384]{0:T(512)}, /*index=5*/f32[3...) custom-call(bf16[128,768]{1,0:T(8,128)(2,1)} %get-tuple-element.36.r, ...), custom_call_target="tpu_custom_call" | custom-call | tf_op jit(solution)/shard_map/unpack/pallas_call | solution.py:1276

commit v3 on v2

--- a/solution.py
+++ b/solution.py
@@ -565,11 +565,9 @@
     att_copy = remote(b.att2.at[near_tokens], b.att2.at[far_tokens], s.ex, 3, at.across)
     start(att_copy)
     start(dout_copy)
-    sister_arrivals(1)
-    relay_rest(3)
-    own_copies[1].wait()
-    tok_copy.wait_recv()
-    att_copy.wait_recv()
+    for w in (1, 2):
+        own_copies[w].wait()
+        sister_arrivals(w)
 
     def normalise(hidden):
         center = hidden - jnp.mean(hidden, -1, keepdims=True)
@@ -587,33 +585,43 @@
     def column_sum(value):
         return jnp.sum(value, axis=0, keepdims=True)
 
-    first = (
-        b.tok2[...].astype(F32)
-        + jnp.dot(b.att2[...], b.wo[...], preferred_element_type=F32)
-        + bias[2:3]
-    )
-    unit_one, inverse_one = normalise(first)
-    b.unit_one[...] = unit_one
-    normed = unit_one * bias[3:4] + bias[4:5]
-    b.norm_low[...] = normed.astype(BF16)
-    b.second[...] = normed + bias[9:10]
-    relay_diagonal(3)
-    for w in (2, 3):
-        own_copies[w].wait()
-        sister_arrivals(w)
-    for c in range(4):
-        cols = slice(c * MODEL, (c + 1) * MODEL)
-        part = halves[c // 2]
-        i = 5 + 2 * (c % 2)
-        line = jnp.concatenate([part[i : i + 1], part[i + 1 : i + 2]], axis=1)
-        inner = jnp.dot(b.norm_low[...], b.wi[:, cols], preferred_element_type=F32) + line
-        gate = 0.5 * (1.0 + lax.erf(inner * ROOT_HALF))
-        activation = (inner * gate).astype(BF16)
-        b.act[:, cols] = activation
-        b.slope[c * BOTH : (c + 1) * BOTH, :] = (
-            gate + inner * jnp.exp(-0.5 * inner * inner) * INV_ROOT_TAU
-        )
-        b.second[...] += jnp.dot(activation, b.wb[cols, :], preferred_element_type=F32)
+    def dense_forward(side):
+        lines = (near_tokens, far_tokens)[side]
+        first = (
+            b.tok2[lines, :].astype(F32)
+            + jnp.dot(b.att2[lines, :], b.wo[...], preferred_element_type=F32)
+            + bias[2:3]
+        )
+        unit, inverse = normalise(first)
+        b.unit_one[lines, :] = unit
+        normed = unit * bias[3:4] + bias[4:5]
+        b.norm_low[lines, :] = normed.astype(BF16)
+        b.second[lines, :] = normed + bias[9:10]
+        for c in range(4):
+            if side == 1 and c == 2:
+                relay_diagonal(3)
+            cols = slice(c * MODEL, (c + 1) * MODEL)
+            part = halves[c // 2]
+            i = 5 + 2 * (c % 2)
+            line = jnp.concatenate([part[i : i + 1], part[i + 1 : i + 2]], axis=1)
+            inner = line + jnp.dot(
+                b.norm_low[lines, :], b.wi[:, cols], preferred_element_type=F32
+            )
+            gate = 0.5 * (1.0 + lax.erf(inner * ROOT_HALF))
+            b.act[lines, cols] = (inner * gate).astype(BF16)
+            b.slope[pl.ds(c * BOTH + side * BLOCK, BLOCK), :] = (
+                gate + inner * jnp.exp(-0.5 * inner * inner) * INV_ROOT_TAU
+            )
+        return inverse
+
+    near_inverse = dense_forward(0)
+    relay_rest(3)
+    tok_copy.wait_recv()
+    att_copy.wait_recv()
+    inverse_one = jnp.concatenate([near_inverse, dense_forward(1)], axis=0)
+    own_copies[3].wait()
+    sister_arrivals(3)
+    b.second[...] += jnp.dot(b.act[...], b.wb[...], preferred_element_type=F32)
     unit_two, inverse_two = normalise(b.second[...])
     b.result[...] = (unit_two[:BLOCK] * bias[10:11] + bias[11:12]).astype(BF16)
     dout_copy.wait_recv()
@@ -698,7 +706,7 @@
 
     def each_owner(group, act, span):
         def one(d, carry):
-            j = (at.p + d) % planes
+            j = jnp.where(at.p < planes // 2, planes - d, d - 1)
 
             @pl.when(j < owners[group])
             def _():
@@ -734,7 +742,7 @@
             of("y_send", group)[lines, :] = (
                 out_quarter(at.peer(2)) + come[0, lines, :].astype(F32)
             ).astype(BF16)
-        go_over_y(group, early)
+        go_over_y(group, (1, 2) if group == 0 else early)
         core_copy(group, 1).wait_recv()
         used = SET_ROWS[0] if group == 0 else HALF + QUARTER
         b.slope[base : base + used, :] += come[1, 0:used, :].astype(F32)
@@ -915,7 +923,7 @@
                 b.dsend.at[g], b.do.at[block_rows(0, at.r)], s.a2a, (4, d), at.in_plane(g)
             )
         )
-    go_over_y(0, late)
+    go_over_y(0, (2, planes + 1))
     b.do[block_rows(0, at.r), :] = b.dsend[at.r]
 
     for j in range(3):
@@ -924,6 +932,7 @@
         b.att2[:, pl.ds(near_rows, HALF)], b.d_first[...], TN, preferred_element_type=F32
     )
     make(1)
+    scatter(0, (1, 2))
 
     b.grads[...] = jnp.zeros_like(b.grads)
     b.dq[...] = jnp.zeros_like(b.dq)
@@ -966,7 +975,6 @@
 
     down_grads = remote(b.halo_send.at[0], b.halo.at[1], s.halo_b, 0, at.down)
     up_grads = remote(b.halo_send.at[1], b.halo.at[0], s.halo_b, 1, at.up)
-    scatter(0, early)
     visit_plane(0)
     b.halo_send[0] = b.grads[pl.ds(0, PLANE), :].astype(BF16)
 
@@ -974,6 +982,7 @@
     def _():
         down_grads.start()
 
+    scatter(0, (2, 3))
     exchange(1)
     visit_plane(2)
     b.halo_send[1] = b.grads[pl.ds(2 * PLANE, PLANE), :].astype(BF16)
@@ -982,16 +991,19 @@
     def _():
         up_grads.start()
 
-    scatter(0, late)
     go_over_y(1, late)
+    scatter(0, (3, planes + 1))
+    relay_sums(0, 1)
     visit_plane(1)
     b.d_group[:, 0:256] = b.dq[...].astype(BF16)
-    relay_sums(0, 1)
 
     @pl.when(at.has_up)
     def _():
         remote(b.halo.at[1], b.halo.at[1], s.halo_b, 0, at.up).wait_recv()
         b.grads[pl.ds(PLANE, PLANE), :] += b.halo[1].astype(F32)
+
+    relay_sums(0, 2)
+    scatter(1, early)
 
     @pl.when(at.has_down)
     def _():
@@ -1035,8 +1047,6 @@
         small_copy(i).wait()
         b.small[...] += b.small_recv[i]
 
-    relay_sums(0, 2)
-    scatter(1, early)
     more_sums(0)
     settle(0)
     line_copy.wait_recv()
@@ -1044,10 +1054,10 @@
     mine = lax.broadcasted_iota(jnp.int32, (8, 640), 0) == at.r
     b.small[16:24, 0:640] = jnp.where(mine, line, 0.0)
     small_copy(0).start()
+    small_finish(0)
+    small_copy(1).start()
     scatter(1, late)
     relay_sums(1, 1)
-    small_finish(0)
-    small_copy(1).start()
     come_in(0, 1)
     scatter(2, early)
     relay_sums(1, 2)

time: 168 us -> 162 us (0.964)
  Pallas kernels: 167 us -> 161 us
    pallas_call x1, Pallas kernels: 157 us -> 152 us  [layer_call(): pl.pallas_call(functools.partial(layer_kernel, planes, list(buffers), lis...]
where the time goes in v3:
time: 162 us
  Pallas kernels  161 us (99%)
    pallas_call x1, Pallas kernels, layer_call(): pl.pallas_call(functools.partial(layer_kernel, planes, list(buffers), lis...  152 us
    pallas_call x1, Pallas kernels, unpack_call(): pl.pallas_call(unpack_kernel, out_shape=[o[0] for o in outs], in_specs=[v...  9.86 us

profile of v3, /device:TPU:0, one launch (start us, length us, event | category | flops | bytes accessed | tf_op | source)
XLA Modules:
  0.0 162.2 jit_solution(7718561800159585898)
XLA Ops:
  0.7 151.5 %layer.1 = (bf16[128,768]{1,0:T(8,128)(2,1)}, f32[128,768]{1,0:T(8,128)}, bf16[1536,768]{1,0:T(8,128)(2,1)}, bf16[2048,768]{1,0:T(8,128)(2,1)}, bf16[1536,640]{1,0:T(8,128)(2,1)}, /*index=5*/f32[24,768]{1,0:T(8,128)}) custom-call(bf16[1,128,768]{2,1,0:T(8,128)(2,1)} %refs_0_.1, s32[1,128]{1,0:T(1,128)} %refs_1_.1, bf16[384,2304]{1,0:T(8,128)(2,1)} %refs_2_.1, ...), custom_call_target="tpu_custom_call" | custom-call | tf_op jit(solution)/shard_map/layer/pallas_call | solution.py:1176
  152.2 9.9 %unpack.1 = (bf16[128,768]{1,0:T(8,128)(2,1)}, f32[128,768]{1,0:T(8,128)}, f32[384,2304]{1,0:T(8,128)}, f32[384]{0:T(512)}, f32[384]{0:T(512)}, /*index=5*/f32[3...) custom-call(bf16[128,768]{1,0:T(8,128)(2,1)} %get-tuple-element.36.r, ...), custom_call_target="tpu_custom_call" | custom-call | tf_op jit(solution)/shard_map/unpack/pallas_call | solution.py:1286

commit v4 on v3

--- a/solution.py
+++ b/solution.py
@@ -154,8 +154,8 @@
         halo_send=((2, PLANE, 2 * LANES), BF16),
         halo=((2, PLANE, 2 * LANES), BF16),
         d_group=((PLANE, 640), BF16),
-        d_recv=((GROUP, BLOCK, 640), BF16),
-        d_packed=((BLOCK, 3 * MODEL), BF16),
+        dt_send=((3, BLOCK, MODEL), BF16),
+        dt_recv=((3, BLOCK, MODEL), BF16),
         q_sum=((HALF, 640), F32),
         x_send=((HALF, 640), BF16),
         x_recv=((HALF, 640), BF16),
@@ -175,20 +175,19 @@
         buffers[f"down_recv{g}"] = ((rows, width), BF16)
         buffers[f"final{g}"] = ((chunk, width), BF16)
     semaphores = dict(
-        local=(4 + 3,),
+        local=(4,),
         qx=(3,),
         qz=(3,),
         qc=(2, 3),
-        late_x=(3,),
-        late_c=(3,),
-        wx=(4, 2),
-        wy=(4, 2),
-        wz=(4, 2),
-        wc=(4, 5),
+        dt=(3,),
+        wx=(5,),
+        wy=(4,),
+        wz=(4,),
+        wc=(13,),
         ex=(5,),
-        tp=(4,),
-        a2a=(6, 4),
-        halo_f=(2, 5),
+        tp=(3,),
+        a2a=(3, 3),
+        halo_f=(2, 2),
         halo_b=(2,),
         core=(4,),
         xs=(planes,),
@@ -282,13 +281,19 @@
             shards[w].at[pl.ds(first, size)],
             wholes[w].at[pl.ds(pl.multiple_of(base + first, 16), size)],
             s.wx,
-            (w, i),
+            2 * (w - 1) + i,
             at.across,
         )
 
     def piece_copy(w, quarter, sems, index, device, part=None, core=None):
         piece = far(w, quarter, at.k if core is None else core, part)
-        return remote(piece, piece, sems, (w, index), device)
+        if sems is s.wx:
+            slot = 2 * (w - 1) + index
+        elif sems is s.wc:
+            slot = 12 if index == 4 else 4 * (w - 1) + index
+        else:
+            slot = 3 if index else w - 1
+        return remote(piece, piece, sems, slot, device)
 
     def relay_own(w):
         piece_copy(w, own_q, s.wx, 0, at.across).wait_recv()
@@ -357,20 +362,6 @@
         piece = q_piece(b.wq, far_base + q_rows(core, parity), QUARTER, j, at.y)
         return remote(piece, piece, sems, index, device)
 
-    def late_across(j):
-        line = at.k * 2 * QUARTER
-        return remote(
-            q_piece(b.w_qkv, line, 2 * QUARTER, j, 1 - at.y),
-            q_piece(b.wq, near_base + line, 2 * QUARTER, j, 1 - at.y),
-            s.late_x,
-            j,
-            at.across,
-        )
-
-    def late_move(core, j, sems, device):
-        piece = q_piece(b.wq, far_base + core * 2 * QUARTER, 2 * QUARTER, j, 1 - at.y)
-        return remote(piece, piece, sems, j, device)
-
     def tok_block(i, sem, device):
         piece = b.tok_plane.at[block_rows(0, i)]
         return remote(piece, piece, s.tp, sem, device)
@@ -393,7 +384,7 @@
     own_copies[0].start()
     for d in (1, 2, 3):
         mine = b.ids.at[1, at.r]
-        start(remote(mine, mine, s.a2a, (0, d), at.in_plane(at.peer(d))))
+        start(remote(mine, mine, s.a2a, (0, d - 1), at.in_plane(at.peer(d))))
 
     near_rows = pl.multiple_of(at.x * HALF, HALF)
     far_rows = pl.multiple_of((1 - at.x) * HALF, HALF)
@@ -471,7 +462,7 @@
     down_ids = remote(b.ids.at[1], b.ids.at[2], s.halo_f, (1, 1), at.down)
 
     def from_peer(piece, kind, d):
-        remote(piece, piece, s.a2a, (kind, d), at.in_plane(at.peer(d))).wait_recv()
+        remote(piece, piece, s.a2a, (kind, d - 1), at.in_plane(at.peer(d))).wait_recv()
 
     both_ways(up_kv, down_kv, go)
     b.qp[...] = jnp.concatenate(
@@ -552,13 +543,13 @@
 
     for d in (1, 2, 3):
         i = at.peer(d)
-        start(remote(b.asend.at[i], b.arecv.at[at.r], s.a2a, (3, d), at.in_plane(i)))
+        start(remote(b.asend.at[i], b.arecv.at[at.r], s.a2a, (1, d - 1), at.in_plane(i)))
     b.arecv[at.r] = b.asend[at.r]
     relay_own(3)
     relay_rest(1)
     relay_rest(2)
     for d in (1, 2, 3):
-        from_peer(b.arecv.at[at.peer(d)], 3, d)
+        from_peer(b.arecv.at[at.peer(d)], 1, d)
     b.att2[near_tokens, :] = jnp.concatenate(
         [b.arecv[g].astype(F32)[:, HEAD_DIM : HEAD_DIM + LANES] for g in range(GROUP)], axis=1
     ).astype(BF16)
@@ -836,7 +827,7 @@
 
     def settle_copy(group):
         return pltpu.make_async_copy(
-            of("final", group), place(group, at.r, at.p), s.local[0].at[4 + group]
+            of("final", group), place(group, at.r, at.p), s.local[1].at[group]
         )
 
     def settle(group):
@@ -920,14 +911,12 @@
         g = at.peer(d)
         start(
             remote(
-                b.dsend.at[g], b.do.at[block_rows(0, at.r)], s.a2a, (4, d), at.in_plane(g)
+                b.dsend.at[g], b.do.at[block_rows(0, at.r)], s.a2a, (2, d - 1), at.in_plane(g)
             )
         )
     go_over_y(0, (2, planes + 1))
     b.do[block_rows(0, at.r), :] = b.dsend[at.r]
 
-    for j in range(3):
-        start(late_across(j))
     b.out_tile[...] = lax.dot_general(
         b.att2[:, pl.ds(near_rows, HALF)], b.d_first[...], TN, preferred_element_type=F32
     )
@@ -937,7 +926,7 @@
     b.grads[...] = jnp.zeros_like(b.grads)
     b.dq[...] = jnp.zeros_like(b.dq)
     for d in (1, 2, 3):
-        from_peer(b.do.at[block_rows(0, at.peer(d))], 4, d)
+        from_peer(b.do.at[block_rows(0, at.peer(d))], 2, d)
     do_t = b.do[...].astype(F32).T
     for h in range(GROUP_HEADS):
         lines = slice(HEAD_DIM * (h + 1), HEAD_DIM * (h + 2))
@@ -1019,21 +1008,10 @@
         b.tok_plane[:, pl.ds(far_rows, HALF)], b.d_group[...], TN, preferred_element_type=F32
     ).astype(BF16)
     each_owner(2, lambda j: x_copy(j).start(), whole_way)
-    for d in (1, 2, 3):
-        i = at.peer(d)
-        start(
-            remote(
-                b.d_group.at[block_rows(0, i)],
-                b.d_recv.at[at.r],
-                s.a2a,
-                (5, d),
-                at.in_plane(i),
-            )
-        )
-    b.d_recv[at.r] = b.d_group[block_rows(0, at.r), :]
     b.q_sum[...] = lax.dot_general(
         b.tok_plane[:, pl.ds(near_rows, HALF)], b.d_group[...], TN, preferred_element_type=F32
     )
+
     partners = [at.sister, at.beside]
     span = 1
     while span < planes:
@@ -1047,122 +1025,153 @@
         small_copy(i).wait()
         b.small[...] += b.small_recv[i]
 
+    def sums_sent(group):
+        def one(j, carry):
+            if group == 2:
+                x_copy(j).wait_send()
+            else:
+                y_copy(group, j).wait_send()
+
+            @pl.when(at.p < j)
+            def _():
+                up_copy(group, j).wait_send()
+
+            @pl.when(at.p > j)
+            def _():
+                down_copy(group, j).wait_send()
+
+            return carry
+
+        lax.fori_loop(0, owners[group], one, 0)
+
+        @pl.when(at.p < owners[group])
+        def _():
+            settle_copy(group).wait()
+
+    def gathers_done(group):
+        def one(j, carry):
+            gather_copy(group, at.peer(1), j, s.gc, at.sister).wait_recv()
+            gather_copy(group, at.peer(3), j, s.gf, at.sister).wait_recv()
+            gather_copy(group, at.r, j, s.gy, at.beside).wait_send()
+            gather_copy(group, at.r, j, s.gc, at.sister).wait_send()
+            gather_copy(group, at.peer(2), j, s.gf, at.sister).wait_send()
+
+            @pl.when(jnp.logical_and(j <= at.p, at.has_up))
+            def _():
+                gather_copy(group, at.r, j, s.gu, at.up).wait_send()
+
+            @pl.when(jnp.logical_and(j >= at.p, at.has_down))
+            def _():
+                gather_copy(group, at.r, j, s.gd, at.down).wait_send()
+
+            return carry
+
+        lax.fori_loop(0, owners[group], one, 0)
+
+    def finish(copy):
+        copy.wait_send()
+
     more_sums(0)
     settle(0)
+    relay_sums(1, 1)
     line_copy.wait_recv()
     line = b.line_send[...] + b.line_recv[...]
     mine = lax.broadcasted_iota(jnp.int32, (8, 640), 0) == at.r
     b.small[16:24, 0:640] = jnp.where(mine, line, 0.0)
     small_copy(0).start()
+    scatter(2, early)
     small_finish(0)
     small_copy(1).start()
     scatter(1, late)
-    relay_sums(1, 1)
+
+    spare = 2 * BOTH
+    gap = jnp.zeros((PLANE, HEAD_DIM), F32)
+    for j, first_lane in enumerate((0, 256, 448)):
+        piece = b.d_group[...].astype(F32)[:, first_lane : first_lane + LANES]
+        wide = jnp.where(
+            at.k == 0,
+            jnp.concatenate([piece, gap], axis=1),
+            jnp.concatenate([gap, piece], axis=1),
+        ).astype(BF16)
+        part = lax.dot_general(wide, b.wq[:, window[j]], NT, preferred_element_type=F32)
+        if j == 0:
+            b.slope[spare : spare + PLANE, :] = part
+        else:
+            b.slope[spare : spare + PLANE, :] += part
+
+    def dt_block(i):
+        return b.slope[block_rows(spare, i), :]
+
+    def dt_copy(i):
+        device = at.beside if i == 2 else at.sister
+        return remote(b.dt_send.at[i], b.dt_recv.at[i], s.dt, i, device)
+
+    for i, block in enumerate((at.peer(3), at.peer(1))):
+        b.dt_send[i] = dt_block(block).astype(BF16)
+        start(dt_copy(i))
+
     come_in(0, 1)
-    scatter(2, early)
     relay_sums(1, 2)
+    relay_sums(2, 1)
     hand_over(0, 0)
     scatter(2, late)
-    relay_sums(2, 1)
-    come_in(0, 2)
+    relay_sums(2, 2)
+    dt_copy(0).wait_recv()
+    b.dt_send[2] = (dt_block(at.peer(2)) + b.dt_recv[0].astype(F32)).astype(BF16)
+    start(dt_copy(2))
     more_sums(1)
     settle(1)
-    relay_sums(2, 2)
+    come_in(0, 2)
     more_sums(2)
+    settle(2)
     small_finish(1)
     small_copy(2).start()
-    for j in range(3):
-        late_move(at.k, j, s.late_x, at.across).wait_recv()
-        start(late_move(at.k, j, s.late_c, at.sister))
     hand_over(0, 1)
+    come_in(1, 1)
     come_in(0, 3)
-    settle(2)
-    come_in(1, 1)
+    come_in(2, 1)
+    for copy in sent:
+        copy.wait_send()
+    both_ways(up_kv, down_kv, finish)
+    both_ways(up_ids, down_ids, finish)
+    both_ways(up_grads, down_grads, finish)
+    for group in range(3):
+        sums_sent(group)
+    hand_over(0, 2)
+    dt_copy(1).wait_recv()
+    dt_copy(2).wait_recv()
+    b.d_tokens[...] += (
+        dt_block(at.r) + b.dt_recv[1].astype(F32) + b.dt_recv[2].astype(F32)
+    )
+    come_in(1, 2)
+    come_in(2, 2)
     small_finish(2)
     small_copy(3).start()
-    hand_over(0, 2)
-
-    for d in (1, 2, 3):
-        from_peer(b.d_recv.at[at.peer(d)], 5, d)
-    for j, first_lane in enumerate((0, 256, 448)):
-        b.d_packed[:, j * MODEL : (j + 1) * MODEL] = jnp.concatenate(
-            [
-                b.d_recv[g].astype(F32)[:, first_lane : first_lane + LANES]
-                for g in range(GROUP)
-            ],
-            axis=1,
-        ).astype(BF16)
-    for j in range(3):
-        late_move(1 - at.k, j, s.late_c, at.sister).wait_recv()
-    b.d_tokens[...] += lax.dot_general(
-        b.d_packed[...], b.wq[...], NT, preferred_element_type=F32
-    )
-    come_in(1, 2)
-    come_in(2, 1)
     hand_over(0, 3)
     hand_over(1, 0)
     come_in(1, 3)
-    come_in(2, 2)
+    come_in(2, 3)
     hand_over(2, 0)
     hand_over(1, 1)
-    come_in(2, 3)
-    small_finish(3)
+    if planes <= GROUP:
+        gathers_done(0)
     hand_over(2, 1)
     hand_over(1, 2)
+    small_finish(3)
     hand_over(2, 2)
     hand_over(1, 3)
+    if planes <= GROUP:
+        gathers_done(1)
     hand_over(2, 3)
     more_gathers()
     for i in range(4, len(partners)):
         small_copy(i).start()
         small_finish(i)
 
-    for group in range(3):
-
-        def last(j, carry, group=group):
-            gather_copy(group, at.peer(1), j, s.gc, at.sister).wait_recv()
-            gather_copy(group, at.peer(3), j, s.gf, at.sister).wait_recv()
-            gather_copy(group, at.r, j, s.gy, at.beside).wait_send()
-            gather_copy(group, at.r, j, s.gc, at.sister).wait_send()
-            gather_copy(group, at.peer(2), j, s.gf, at.sister).wait_send()
-            if group == 2:
-                x_copy(j).wait_send()
-            else:
-                y_copy(group, j).wait_send()
-
-            @pl.when(jnp.logical_and(j <= at.p, at.has_up))
-            def _():
-                gather_copy(group, at.r, j, s.gu, at.up).wait_send()
-
-            @pl.when(jnp.logical_and(j >= at.p, at.has_down))
-            def _():
-                gather_copy(group, at.r, j, s.gd, at.down).wait_send()
-
-            @pl.when(at.p < j)
-            def _():
-                up_copy(group, j).wait_send()
-
-            @pl.when(at.p > j)
-            def _():
-                down_copy(group, j).wait_send()
-
-            return carry
-
-        lax.fori_loop(0, owners[group], last, 0)
-
-        @pl.when(at.p < owners[group])
-        def _(group=group):
-            settle_copy(group).wait()
-
-    for copy in sent:
-        copy.wait_send()
-
-    def finish(copy):
-        copy.wait_send()
-
-    both_ways(up_kv, down_kv, finish)
-    both_ways(up_ids, down_ids, finish)
-    both_ways(up_grads, down_grads, finish)
+    if planes > GROUP:
+        gathers_done(0)
+        gathers_done(1)
+    gathers_done(2)
 
 
 def layer_call(planes, args):

time: 162 us -> 158 us (0.975)
  Pallas kernels: 161 us -> 157 us
    pallas_call x1, Pallas kernels: 152 us -> 148 us  [layer_call(): pl.pallas_call(functools.partial(layer_kernel, planes, list(buffers), lis...]
where the time goes in v4:
time: 158 us
  Pallas kernels  157 us (99%)
    pallas_call x1, Pallas kernels, layer_call(): pl.pallas_call(functools.partial(layer_kernel, planes, list(buffers), lis...  148 us
    pallas_call x1, Pallas kernels, unpack_call(): pl.pallas_call(unpack_kernel, out_shape=[o[0] for o in outs], in_specs=[v...  9.86 us

profile of v4, /device:TPU:0, one launch (start us, length us, event | category | flops | bytes accessed | tf_op | source)
XLA Modules:
  0.0 158.3 jit_solution(1135282026307693764)
XLA Ops:
  0.7 147.6 %layer.1 = (bf16[128,768]{1,0:T(8,128)(2,1)}, f32[128,768]{1,0:T(8,128)}, bf16[1536,768]{1,0:T(8,128)(2,1)}, bf16[2048,768]{1,0:T(8,128)(2,1)}, bf16[1536,640]{1,0:T(8,128)(2,1)}, /*index=5*/f32[24,768]{1,0:T(8,128)}) custom-call(bf16[1,128,768]{2,1,0:T(8,128)(2,1)} %refs_0_.1, s32[1,128]{1,0:T(1,128)} %refs_1_.1, bf16[384,2304]{1,0:T(8,128)(2,1)} %refs_2_.1, ...), custom_call_target="tpu_custom_call" | custom-call | tf_op jit(solution)/shard_map/layer/pallas_call | solution.py:1185
  148.3 9.9 %unpack.1 = (bf16[128,768]{1,0:T(8,128)(2,1)}, f32[128,768]{1,0:T(8,128)}, f32[384,2304]{1,0:T(8,128)}, f32[384]{0:T(512)}, f32[384]{0:T(512)}, /*index=5*/f32[3...) custom-call(bf16[128,768]{1,0:T(8,128)(2,1)} %get-tuple-element.36.r, ...), custom_call_target="tpu_custom_call" | custom-call | tf_op jit(solution)/shard_map/unpack/pallas_call | solution.py:1295

commit v5 on v4

--- a/solution.py
+++ b/solution.py
@@ -643,8 +643,23 @@
     def out_quarter(t):
         return b.out_tile[pl.ds(pl.multiple_of(t * QUARTER, 16), QUARTER), :]
 
-    def chunk_rows(group, j):
-        return pl.ds(pl.multiple_of(j * chunks[group], 16), chunks[group])
+    def chunk_rows(group, j, size=None):
+        return pl.ds(pl.multiple_of(j * chunks[group], 16), size or chunks[group])
+
+    def trimmed(group, j, act):
+        size, last = chunks[group], owners[group] - 1
+        used = HALF + QUARTER - last * size
+        if group != 1 or not 0 < used < size:
+            act(size)
+            return
+
+        @pl.when(j == last)
+        def _():
+            act(used)
+
+        @pl.when(j != last)
+        def _():
+            act(size)
 
     def own_chunk(group, j):
         if group == 2:
@@ -661,8 +676,8 @@
             at.sister,
         )
 
-    def y_copy(group, j):
-        lines = chunk_rows(group, j)
+    def y_copy(group, j, size):
+        lines = chunk_rows(group, j, size)
         return remote(
             of("y_send", group).at[lines],
             of("y_recv", group).at[lines],
@@ -671,8 +686,8 @@
             at.beside,
         )
 
-    def up_copy(group, j):
-        lines = chunk_rows(group, j)
+    def up_copy(group, j, size):
+        lines = chunk_rows(group, j, size)
         return remote(
             of("z_send", group).at[lines],
             of("up_recv", group).at[lines],
@@ -681,8 +696,8 @@
             at.up,
         )
 
-    def down_copy(group, j):
-        lines = chunk_rows(group, j)
+    def down_copy(group, j, size):
+        lines = chunk_rows(group, j, size)
         return remote(
             of("z_send", group).at[lines],
             of("down_recv", group).at[lines],
@@ -718,8 +733,11 @@
         if group == 1:
             b.slope[base + HALF : base + HALF + QUARTER, :] = out_quarter(at.r)
 
-    def go_over_y(group, span):
-        each_owner(group, lambda j: y_copy(group, j).start(), span)
+    def go_trimmed(group, span):
+        def act(j):
+            trimmed(group, j, lambda size: y_copy(group, j, size).start())
+
+        each_owner(group, act, span)
 
     def exchange(group):
         base = OWN_ROWS[group]
@@ -733,7 +751,7 @@
             of("y_send", group)[lines, :] = (
                 out_quarter(at.peer(2)) + come[0, lines, :].astype(F32)
             ).astype(BF16)
-        go_over_y(group, (1, 2) if group == 0 else early)
+        go_trimmed(group, (1, 2) if group == 0 else early)
         core_copy(group, 1).wait_recv()
         used = SET_ROWS[0] if group == 0 else HALF + QUARTER
         b.slope[base : base + used, :] += come[1, 0:used, :].astype(F32)
@@ -745,7 +763,7 @@
                 x_copy(j).wait_recv()
                 came = b.x_recv[chunk_rows(2, j), :]
             else:
-                y_copy(group, j).wait_recv()
+                trimmed(group, j, lambda size: y_copy(group, j, size).wait_recv())
                 came = of("y_recv", group)[chunk_rows(group, j), :]
             total = mine[...] + came.astype(F32)
             mine[...] = total
@@ -753,20 +771,22 @@
             @pl.when(jnp.logical_and(at.p == 0, j > 0))
             def _():
                 of("z_send", group)[chunk_rows(group, j), :] = total.astype(BF16)
-                up_copy(group, j).start()
+                trimmed(group, j, lambda size: up_copy(group, j, size).start())
 
             @pl.when(jnp.logical_and(at.p == planes - 1, j < planes - 1))
             def _():
                 of("z_send", group)[chunk_rows(group, j), :] = total.astype(BF16)
-                down_copy(group, j).start()
+                trimmed(group, j, lambda size: down_copy(group, j, size).start())
 
         each_owner(group, act, span)
 
     def add_arrived(group, j, name, sems, device):
-        lines = chunk_rows(group, j)
-        came = of(name, group).at[lines]
-        remote(came, came, sems, (group, j), device).wait_recv()
-        return came[...].astype(F32)
+        def wait(size):
+            came = of(name, group).at[chunk_rows(group, j, size)]
+            remote(came, came, sems, (group, j), device).wait_recv()
+
+        trimmed(group, j, wait)
+        return of(name, group)[chunk_rows(group, j), :].astype(F32)
 
     def relay_sums(group, h):
         @pl.when(at.p == h)
@@ -777,7 +797,7 @@
                     group, j, "up_recv", s.up, at.down
                 )
                 of("z_send", group)[chunk_rows(group, j), :] = total.astype(BF16)
-                up_copy(group, j).start()
+                trimmed(group, j, lambda size: up_copy(group, j, size).start())
                 return carry
 
             lax.fori_loop(0, owners[group] - 1 - at.p, one, 0)
@@ -789,7 +809,7 @@
                     group, j, "down_recv", s.down, at.up
                 )
                 of("z_send", group)[chunk_rows(group, j), :] = total.astype(BF16)
-                down_copy(group, j).start()
+                trimmed(group, j, lambda size: down_copy(group, j, size).start())
                 return carry
 
             lax.fori_loop(0, jnp.minimum(at.p, owners[group]), one, 0)
@@ -805,24 +825,39 @@
 
         lax.fori_loop(3, planes - 1, one, 0)
 
-    def place(group, t, j):
+    def place(group, t, j, size=None):
         first_row = t * SET_ROWS[group] + j * chunks[group]
-        return of("sums", group).at[pl.ds(pl.multiple_of(first_row, 16), chunks[group])]
-
-    def gather_copy(group, t, j, sems, device, source=None):
-        piece = place(group, t, j)
-        return remote(piece if source is None else source, piece, sems, (group, j), device)
+        lines = pl.ds(pl.multiple_of(first_row, 16), size or chunks[group])
+        return of("sums", group).at[lines]
+
+    def gather_copy(group, t, j, sems, device, source=None, size=None):
+        piece = place(group, t, j, size)
+        if source is None:
+            source = piece
+        elif size is not None:
+            source = source.at[pl.ds(0, size)]
+        return remote(source, piece, sems, (group, j), device)
+
+    def linked(group, t, j, sems, device, source=None):
+        def copy(size):
+            return gather_copy(group, t, j, sems, device, source, size)
+
+        return types.SimpleNamespace(
+            start=lambda: trimmed(group, j, lambda size: copy(size).start()),
+            wait_recv=lambda: trimmed(group, j, lambda size: copy(size).wait_recv()),
+            wait_send=lambda: trimmed(group, j, lambda size: copy(size).wait_send()),
+        )
 
     def spread(group, j, source=None):
         @pl.when(jnp.logical_and(j <= at.p, at.has_up))
         def _():
-            gather_copy(group, at.r, j, s.gu, at.up, source).start()
+            linked(group, at.r, j, s.gu, at.up, source).start()
 
         @pl.when(jnp.logical_and(j >= at.p, at.has_down))
         def _():
-            gather_copy(group, at.r, j, s.gd, at.down, source).start()
-
-        gather_copy(group, at.r, j, s.gy, at.beside, source).start()
+            linked(group, at.r, j, s.gd, at.down, source).start()
+
+        linked(group, at.r, j, s.gy, at.beside, source).start()
         gather_copy(group, at.r, j, s.gc, at.sister, source).start()
 
     def settle_copy(group):
@@ -859,14 +894,14 @@
 
     def come_in(group, d):
         def act(j, sems, device):
-            gather_copy(group, at.r, j, sems, device).wait_recv()
+            linked(group, at.r, j, sems, device).wait_recv()
             spread(group, j)
 
         around(group, d, act)
 
     def hand_over(group, d):
         def act(j, sems, device):
-            gather_copy(group, at.peer(2), j, s.gy, at.beside).wait_recv()
+            linked(group, at.peer(2), j, s.gy, at.beside).wait_recv()
             gather_copy(group, at.peer(2), j, s.gf, at.sister).start()
 
         around(group, d, act)
@@ -914,7 +949,7 @@
                 b.dsend.at[g], b.do.at[block_rows(0, at.r)], s.a2a, (2, d - 1), at.in_plane(g)
             )
         )
-    go_over_y(0, (2, planes + 1))
+    go_trimmed(0, (2, planes + 1))
     b.do[block_rows(0, at.r), :] = b.dsend[at.r]
 
     b.out_tile[...] = lax.dot_general(
@@ -980,7 +1015,7 @@
     def _():
         up_grads.start()
 
-    go_over_y(1, late)
+    go_trimmed(1, late)
     scatter(0, (3, planes + 1))
     relay_sums(0, 1)
     visit_plane(1)
@@ -1030,15 +1065,15 @@
             if group == 2:
                 x_copy(j).wait_send()
             else:
-                y_copy(group, j).wait_send()
+                trimmed(group, j, lambda size: y_copy(group, j, size).wait_send())
 
             @pl.when(at.p < j)
             def _():
-                up_copy(group, j).wait_send()
+                trimmed(group, j, lambda size: up_copy(group, j, size).wait_send())
 
             @pl.when(at.p > j)
             def _():
-                down_copy(group, j).wait_send()
+                trimmed(group, j, lambda size: down_copy(group, j, size).wait_send())
 
             return carry
 
@@ -1052,17 +1087,17 @@
         def one(j, carry):
             gather_copy(group, at.peer(1), j, s.gc, at.sister).wait_recv()
             gather_copy(group, at.peer(3), j, s.gf, at.sister).wait_recv()
-            gather_copy(group, at.r, j, s.gy, at.beside).wait_send()
+            linked(group, at.r, j, s.gy, at.beside).wait_send()
             gather_copy(group, at.r, j, s.gc, at.sister).wait_send()
             gather_copy(group, at.peer(2), j, s.gf, at.sister).wait_send()
 
             @pl.when(jnp.logical_and(j <= at.p, at.has_up))
             def _():
-                gather_copy(group, at.r, j, s.gu, at.up).wait_send()
+                linked(group, at.r, j, s.gu, at.up).wait_send()
 
             @pl.when(jnp.logical_and(j >= at.p, at.has_down))
             def _():
-                gather_copy(group, at.r, j, s.gd, at.down).wait_send()
+                linked(group, at.r, j, s.gd, at.down).wait_send()
 
             return carry
 

time: 158 us -> 157 us (level)
    pallas_call x1, Pallas kernels: 148 us -> 146 us  [layer_call(): pl.pallas_call(functools.partial(layer_kernel, planes, list(buffers), lis...]
where the time goes in v5:
time: 157 us
  Pallas kernels  156 us (99%)
    pallas_call x1, Pallas kernels, layer_call(): pl.pallas_call(functools.partial(layer_kernel, planes, list(buffers), lis...  146 us
    pallas_call x1, Pallas kernels, unpack_call(): pl.pallas_call(unpack_kernel, out_shape=[o[0] for o in outs], in_specs=[v...  9.86 us

profile of v5, /device:TPU:0, one launch (start us, length us, event | category | flops | bytes accessed | tf_op | source)
XLA Modules:
  0.0 156.5 jit_solution(14301901866692852678)
XLA Ops:
  0.7 145.8 %layer.1 = (bf16[128,768]{1,0:T(8,128)(2,1)}, f32[128,768]{1,0:T(8,128)}, bf16[1536,768]{1,0:T(8,128)(2,1)}, bf16[2048,768]{1,0:T(8,128)(2,1)}, bf16[1536,640]{1,0:T(8,128)(2,1)}, /*index=5*/f32[24,768]{1,0:T(8,128)}) custom-call(bf16[1,128,768]{2,1,0:T(8,128)(2,1)} %refs_0_.1, s32[1,128]{1,0:T(1,128)} %refs_1_.1, bf16[384,2304]{1,0:T(8,128)(2,1)} %refs_2_.1, ...), custom_call_target="tpu_custom_call" | custom-call | tf_op jit(solution)/shard_map/layer/pallas_call | solution.py:1220
  146.5 9.9 %unpack.1 = (bf16[128,768]{1,0:T(8,128)(2,1)}, f32[128,768]{1,0:T(8,128)}, f32[384,2304]{1,0:T(8,128)}, f32[384]{0:T(512)}, f32[384]{0:T(512)}, /*index=5*/f32[3...) custom-call(bf16[128,768]{1,0:T(8,128)(2,1)} %get-tuple-element.36.r, ...), custom_call_target="tpu_custom_call" | custom-call | tf_op jit(solution)/shard_map/unpack/pallas_call | solution.py:1330

commit v6 on v5

--- a/solution.py
+++ b/solution.py
@@ -733,7 +733,7 @@
         if group == 1:
             b.slope[base + HALF : base + HALF + QUARTER, :] = out_quarter(at.r)
 
-    def go_trimmed(group, span):
+    def go_over_y(group, span):
         def act(j):
             trimmed(group, j, lambda size: y_copy(group, j, size).start())
 
@@ -751,7 +751,7 @@
             of("y_send", group)[lines, :] = (
                 out_quarter(at.peer(2)) + come[0, lines, :].astype(F32)
             ).astype(BF16)
-        go_trimmed(group, (1, 2) if group == 0 else early)
+        go_over_y(group, (1, 2) if group == 0 else early)
         core_copy(group, 1).wait_recv()
         used = SET_ROWS[0] if group == 0 else HALF + QUARTER
         b.slope[base : base + used, :] += come[1, 0:used, :].astype(F32)
@@ -949,7 +949,7 @@
                 b.dsend.at[g], b.do.at[block_rows(0, at.r)], s.a2a, (2, d - 1), at.in_plane(g)
             )
         )
-    go_trimmed(0, (2, planes + 1))
+    go_over_y(0, (2, planes + 1))
     b.do[block_rows(0, at.r), :] = b.dsend[at.r]
 
     b.out_tile[...] = lax.dot_general(
@@ -1015,7 +1015,7 @@
     def _():
         up_grads.start()
 
-    go_trimmed(1, late)
+    go_over_y(1, late)
     scatter(0, (3, planes + 1))
     relay_sums(0, 1)
     visit_plane(1)
@@ -1117,7 +1117,6 @@
     scatter(2, early)
     small_finish(0)
     small_copy(1).start()
-    scatter(1, late)
 
     spare = 2 * BOTH
     gap = jnp.zeros((PLANE, HEAD_DIM), F32)
@@ -1145,6 +1144,7 @@
         b.dt_send[i] = dt_block(block).astype(BF16)
         start(dt_copy(i))
 
+    scatter(1, late)
     come_in(0, 1)
     relay_sums(1, 2)
     relay_sums(2, 1)

time: 157 us -> 157 us (level)
  no operation moved by 1% of the time
where the time goes in v6:
time: 157 us
  Pallas kernels  156 us (99%)
    pallas_call x1, Pallas kernels, layer_call(): pl.pallas_call(functools.partial(layer_kernel, planes, list(buffers), lis...  146 us
    pallas_call x1, Pallas kernels, unpack_call(): pl.pallas_call(unpack_kernel, out_shape=[o[0] for o in outs], in_specs=[v...  9.86 us

profile of v6, /device:TPU:0, one launch (start us, length us, event | category | flops | bytes accessed | tf_op | source)
XLA Modules:
  0.0 156.5 jit_solution(11401754666525288211)
XLA Ops:
  0.7 145.8 %layer.1 = (bf16[128,768]{1,0:T(8,128)(2,1)}, f32[128,768]{1,0:T(8,128)}, bf16[1536,768]{1,0:T(8,128)(2,1)}, bf16[2048,768]{1,0:T(8,128)(2,1)}, bf16[1536,640]{1,0:T(8,128)(2,1)}, /*index=5*/f32[24,768]{1,0:T(8,128)}) custom-call(bf16[1,128,768]{2,1,0:T(8,128)(2,1)} %refs_0_.1, s32[1,128]{1,0:T(1,128)} %refs_1_.1, bf16[384,2304]{1,0:T(8,128)(2,1)} %refs_2_.1, ...), custom_call_target="tpu_custom_call" | custom-call | tf_op jit(solution)/shard_map/layer/pallas_call | solution.py:1220
  146.5 9.9 %unpack.1 = (bf16[128,768]{1,0:T(8,128)(2,1)}, f32[128,768]{1,0:T(8,128)}, f32[384,2304]{1,0:T(8,128)}, f32[384]{0:T(512)}, f32[384]{0:T(512)}, /*index=5*/f32[3...) custom-call(bf16[128,768]{1,0:T(8,128)(2,1)} %get-tuple-element.36.r, ...), custom_call_target="tpu_custom_call" | custom-call | tf_op jit(solution)/shard_map/unpack/pallas_call | solution.py:1330
